TPU v7x, 768 devices: a whole 4x8x12 slice. The times are simulated.
768 devices in a mesh: blk: 96 (over x, z, y_hi), rep: 8 (over y_lo, core).
Axes of the slice: x: 4, y: 8 (y_hi: 2, y_lo: 4; y = y_hi * 4 + y_lo), z: 12, core: 2. Of those that a mesh axis runs over, the one named last changes fastest.
Arguments:
- features: bfloat16 [786432, 128], P(('blk', 'rep')), may hold values from -6 to 6
- neighbours: int32 [786432, 10], P(('blk', 'rep')), may hold values from 0 to 5119
- w_self: bfloat16 [128, 512], replicated, may hold values from -0.5 to 0.5
- w_neigh: bfloat16 [128, 512], replicated, may hold values from -0.5 to 0.5
- bias: float32 [512], replicated, may hold values from -4 to 4
- cotangent: bfloat16 [786432, 512], P(('blk', 'rep')), may hold values from -6 to 6
Outputs:
- hidden: bfloat16 [786432, 512], P(('blk', 'rep'))
- grad_x: bfloat16 [786432, 128], P(('blk', 'rep'))
- grad_self: float32 [128, 512], replicated
- grad_neigh: float32 [128, 512], replicated
- grad_bias: float32 [512], replicated
Inputs may be any that keep to these rules, and one draw needn't show every extreme that they name: `neighbours`: A value v refers to loop position 4 or fewer steps back: v // 1024 steps.
All inputs are finite; a program needn't handle non-finite values.
Results may differ from a plain program's by a relative error of at most 0.007.
Values may be sent and summed in bfloat16 or wider, within the bound.
No kernel may reach another device: no remote copies, remote signals or barrier semaphores. Data moves between devices by JAX's collectives and lax.ppermute only.
A program may use at most 32 MiB of HBM per device.

v0:
```python
import jax
import jax.numpy as jnp
from jax import lax
from jax.sharding import PartitionSpec as P

FAN = 10
STEPS = 4


def shifted(array, axis, by):
    peers = lax.axis_size(axis)
    return lax.ppermute(array, axis, [(i, (i + by) % peers) for i in range(peers)])


def count_tile(near, back, rows):
    target = lax.iota(jnp.int32, rows) + back * rows
    count = jnp.zeros((near.shape[0], rows), jnp.bfloat16)
    for entry in range(near.shape[1]):
        count = count + (near[:, entry][:, None] == target[None, :]).astype(jnp.bfloat16)
    return count


def shards(features, neighbours, w_self, w_neigh, bias, cotangent):
    rows = features.shape[0]
    tiles = [count_tile(neighbours, back, rows) for back in range(STEPS + 1)]
    blocks = [features]
    for back in range(1, STEPS + 1):
        blocks.append(shifted(features, "blk", back))
    total = jnp.zeros((rows, features.shape[1]), jnp.float32)
    for back in range(STEPS + 1):
        total = total + jnp.dot(tiles[back], blocks[back], preferred_element_type=jnp.float32)
    mean = (total / FAN).astype(jnp.bfloat16)
    pre = (
        jnp.dot(features, w_self, preferred_element_type=jnp.float32)
        + jnp.dot(mean, w_neigh, preferred_element_type=jnp.float32)
        + bias
    )
    sig = jax.nn.sigmoid(pre)
    hidden = (pre * sig).astype(jnp.bfloat16)
    dpre = (cotangent.astype(jnp.float32) * sig * (1.0 + pre * (1.0 - sig))).astype(jnp.bfloat16)
    contract = (((0,), (0,)), ((), ()))
    term_self = lax.dot_general(features, dpre, contract, preferred_element_type=jnp.float32)
    term_neigh = lax.dot_general(mean, dpre, contract, preferred_element_type=jnp.float32)
    term_bias = jnp.sum(dpre.astype(jnp.float32), axis=0)
    g_self, g_neigh, g_bias = lax.psum((term_self, term_neigh, term_bias), ("blk", "rep"))
    scale = 1.0 / (rows * lax.axis_size("blk") * lax.axis_size("rep")) ** 0.5
    dself = jnp.dot(dpre, w_self.T, preferred_element_type=jnp.float32)
    dmean = (jnp.dot(dpre, w_neigh.T, preferred_element_type=jnp.float32) / FAN).astype(
        jnp.bfloat16
    )
    local_part = lax.dot_general(tiles[0], dmean, contract, preferred_element_type=jnp.float32)
    grad_x = dself + local_part
    for back in range(1, STEPS + 1):
        remote = lax.dot_general(tiles[back], dmean, contract, preferred_element_type=jnp.float32)
        grad_x = grad_x + shifted(remote.astype(jnp.bfloat16), "blk", -back).astype(remote.dtype)
    return (hidden, grad_x.astype(jnp.bfloat16), g_self * scale, g_neigh * scale, g_bias * scale)


def solution(mesh):
    in_specs = (
        P(("blk", "rep"), None),
        P(("blk", "rep"), None),
        P(),
        P(),
        P(),
        P(("blk", "rep"), None),
    )
    out_specs = (P(("blk", "rep"), None), P(("blk", "rep"), None), P(), P(), P())
    return jax.shard_map(shards, mesh=mesh, in_specs=in_specs, out_specs=out_specs, check_vma=False)
```

profile of v0, /device:TPU:1, one launch (start us, length us, event | category | flops | bytes accessed | tf_op | source)
XLA Modules:
  0.0 580.2 jit_solution(15235288250566564322)
XLA Ops:
  7.2 8.3 %collective-permute-start = (bf16[1024,128]{1,0:T(8,128)(2,1)}, bf16[1024,128]{1,0:T(8,128)(2,1)S(1)}, u32[]{:S(2)}, u32[]{:S(2)}) collective-permute-start(bf16[1024,128]{1,0:T(8,128)(2,1)} %param.6), channel_id=1, source_target_pairs={{0,8},{8,16},{16,24},{24,32},{32,40},{40,48},{48,56},{56,64},{64,7... | collective-permute-start | bytes 786440 | tf_op jit(solution)/shard_map/ppermute | solution.py:12
  15.5 5.8 %collective-permute-start.3 = (bf16[1024,128]{1,0:T(8,128)(2,1)}, bf16[1024,128]{1,0:T(8,128)(2,1)S(1)}, u32[]{:S(2)}, u32[]{:S(2)}) collective-permute-start(bf16[1024,128]{1,0:T(8,128)(2,1)} %param.6), channel_id=1, source_target_pairs={{0,32},{8,40},{16,48},{24,56},{32,64},{40,72},{48,80},{56,88},{64,... | collective-permute-start | bytes 786440 | tf_op jit(solution)/shard_map/ppermute | solution.py:12
  21.3 6.6 %collective-permute-start.2 = (bf16[1024,128]{1,0:T(8,128)(2,1)}, bf16[1024,128]{1,0:T(8,128)(2,1)S(1)}, u32[]{:S(2)}, u32[]{:S(2)}) collective-permute-start(bf16[1024,128]{1,0:T(8,128)(2,1)} %param.6), channel_id=1, source_target_pairs={{0,24},{8,32},{16,40},{24,48},{32,56},{40,64},{48,72},{56,80},{64,... | collective-permute-start | bytes 786440 | tf_op jit(solution)/shard_map/ppermute | solution.py:12
  27.9 4.0 collective-permute-start.1
  32.0 1.1 fusion.74
  33.1 6.4 %fusion.62 = f32[1024,128]{1,0:T(8,128)S(1)} fusion(bf16[1024,128]{1,0:T(8,128)(2,1)} %param.6, s32[1024]{0:T(1024)S(1)} %bitcast.114, s32[1024]{0:T(1024)S(1)} %bitcast.124, s32[1024]{0:T(1024)S(1)} %bitcast.44, s32[1024]{0:T(1024)S(1)} %bitcast.54, s32[1024]{0:T(1024)S(1)} %bitcast.64, s32[1024]{0:T(1024)S(1)} %bitcast.74, s32[1024]{0:T(1024)S(1)} %bitcast.84, ...), kind=kOutput, calls=%fused_computation.126 | convolution fusion | flops 310378496 | bytes 827392 | tf_op jit(solution)/shard_map/dot_general | solution.py:31
  39.9 1.5 collective-permute-done
  41.5 4.3 convolution_add_fusion.2
  45.7 4.6 fusion.65
  50.4 8.5 %collective-permute-done.2 = bf16[1024,128]{1,0:T(8,128)(2,1)S(1)} collective-permute-done((bf16[1024,128]{1,0:T(8,128)(2,1)}, bf16[1024,128]{1,0:T(8,128)(2,1)S(1)}, u32[]{:S(2)}, u32[]{:S(2)}) %collective-permute-start.2) | collective-permute-done | bytes 262176 | tf_op jit(solution)/shard_map/ppermute | solution.py:12
  58.9 4.2 fusion.68
  63.1 5.9 %fusion.58 = bf16[1024,128]{1,0:T(8,128)(2,1)S(1)} fusion(f32[1024,128]{1,0:T(8,128)S(1)} %fusion.65, f32[1024,128]{1,0:T(8,128)S(1)} %fusion.68, f32[1024,128]{1,0:T(8,128)S(1)} %convolution_add_fusion.2, bf16[1024,128]{1,0:T(8,128)(2,1)S(1)} %collective-permute-done.1, s32[1024]{0:T(1024)S(1)} %iota_add_fusion.2, s32[1024]{0:T(1024)S(1)} %bitcast.118, ...), kind=kOutput, calls=%fused_computation.117 | convolution fusion | flops 299499520 | bytes 2142208 | tf_op jit(solution)/shard_map/dot_general | solution.py:31
  69.1 2.3 convert_reduce_fusion
  71.4 1.2 fusion.76
  72.6 1.2 convolution_bitcast_fusion
  73.8 0.4 fusion.59
  74.2 5.7 convolution_convert_fusion.3
  79.9 5.9 %convolution_convert_fusion.2 = bf16[1024,128]{1,0:T(8,128)(2,1)} fusion(bf16[1024,128]{1,0:T(8,128)(2,1)S(1)} %fusion.59, s32[1024]{0:T(1024)S(1)} %iota_add_fusion.2, s32[1024]{0:T(1024)S(1)} %bitcast.120, s32[1024]{0:T(1024)S(1)} %bitcast.130, s32[1024]{0:T(1024)S(1)} %bitcast.50, s32[1024]{0:T(1024)S(1)} %bitcast.60, s32[1024]{0:T(1024)S(1)} %bitcast.70, ...), kind=kOutput, calls=%fused_computation.121 | convolution fusion | flops 298975232 | bytes 569344 | tf_op jit(solution)/shard_map/dot_general | solution.py:54
  85.9 5.7 convolution_convert_fusion.1
  91.6 5.7 convolution_convert_fusion
  97.3 5.8 %fusion.60 = f32[1024,128]{1,0:T(8,128)S(1)} fusion(bf16[1024,128]{1,0:T(8,128)(2,1)S(1)} %fusion.59, s32[1024]{0:T(1024)S(1)} %bitcast.123, s32[1024]{0:T(1024)S(1)} %bitcast.133, s32[1024]{0:T(1024)S(1)} %bitcast.53, s32[1024]{0:T(1024)S(1)} %bitcast.63, s32[1024]{0:T(1024)S(1)} %bitcast.73, s32[1024]{0:T(1024)S(1)} %bitcast.83, s32[1024]{0:T(1024)S(1)} %bitcast.93, ...), kind=kOutput, calls=%fused_computation.125 | convolution fusion | flops 310378496 | bytes 827392 | tf_op jit(solution)/shard_map/dot_general | solution.py:51
  103.2 4.8 collective-permute-start.4
  107.9 2.2 collective-permute-start.5
  110.2 5.3 collective-permute-start.6
  115.5 2.7 collective-permute-start.7
  118.2 113.8 %psum.23 = f32[512]{0:T(512)S(1)} all-reduce(f32[512]{0:T(512)S(1)} %get-tuple-element.12), channel_id=1, replica_groups=mesh['blk'=96,'rep'=8] {'blk','rep'}, use_global_device_ids=true, to_apply=%region_3.0 | all-reduce | flops 512 | bytes 4096 | tf_op jit(solution)/shard_map/psum | solution.py:45
  231.9 0.6 broadcast_multiply_fusion.2
  232.5 336.5 %all-reduce.3.cloned.1.call-done = (f32[128,512]{0,1:T(8,128)}, f32[128,512]{0,1:T(8,128)}) async-done(((f32[128,512]{0,1:T(8,128)}, f32[128,512]{0,1:T(8,128)}), (f32[128,512]{0,1:T(8,128)}, f32[128,512]{0,1:T(8,128)})) %all-reduce.3.cloned.1.call-update) | async-done | bytes 524304 | tf_op jit(solution)/shard_map/psum | solution.py:45
  569.0 1.1 broadcast_multiply_fusion
  570.1 0.8 copy.12
  570.9 0.8 copy.13
  571.8 1.1 add_convert_fusion
  (23 shorter events, 0.6 us)
Async XLA Ops:
  7.2 61.9 %copy-start = (bf16[128,512]{1,0:T(8,128)(2,1)S(1)}, bf16[128,512]{1,0:T(8,128)(2,1)}, u32[]{:S(2)}) copy-start(bf16[128,512]{1,0:T(8,128)(2,1)} %param.9) | copy-start | bytes 393220
  7.2 561.8 %all-reduce.3.cloned.1.call-start = ((), (), s32[]{:S(2)}) async-start(), calls=%async_computation | async-start | bytes 1048576 | tf_op jit(solution)/shard_map/psum | solution.py:45
  7.2 34.2 %collective-permute-start = (bf16[1024,128]{1,0:T(8,128)(2,1)}, bf16[1024,128]{1,0:T(8,128)(2,1)S(1)}, u32[]{:S(2)}, u32[]{:S(2)}) collective-permute-start(bf16[1024,128]{1,0:T(8,128)(2,1)} %param.6), channel_id=1, source_target_pairs={{0,8},{8,16},{16,24},{24,32},{32,40},{40,48},{48,56},{56,64},{64,7... | collective-permute-start | bytes 786440 | tf_op jit(solution)/shard_map/ppermute | solution.py:12
  15.5 30.2 %collective-permute-start.3 = (bf16[1024,128]{1,0:T(8,128)(2,1)}, bf16[1024,128]{1,0:T(8,128)(2,1)S(1)}, u32[]{:S(2)}, u32[]{:S(2)}) collective-permute-start(bf16[1024,128]{1,0:T(8,128)(2,1)} %param.6), channel_id=1, source_target_pairs={{0,32},{8,40},{16,48},{24,56},{32,64},{40,72},{48,80},{56,88},{64,... | collective-permute-start | bytes 786440 | tf_op jit(solution)/shard_map/ppermute | solution.py:12
  21.3 37.6 %collective-permute-start.2 = (bf16[1024,128]{1,0:T(8,128)(2,1)}, bf16[1024,128]{1,0:T(8,128)(2,1)S(1)}, u32[]{:S(2)}, u32[]{:S(2)}) collective-permute-start(bf16[1024,128]{1,0:T(8,128)(2,1)} %param.6), channel_id=1, source_target_pairs={{0,24},{8,32},{16,40},{24,48},{32,56},{40,64},{48,72},{56,80},{64,... | collective-permute-start | bytes 786440 | tf_op jit(solution)/shard_map/ppermute | solution.py:12
  27.9 35.2 %collective-permute-start.1 = (bf16[1024,128]{1,0:T(8,128)(2,1)}, bf16[1024,128]{1,0:T(8,128)(2,1)S(1)}, u32[]{:S(2)}, u32[]{:S(2)}) collective-permute-start(bf16[1024,128]{1,0:T(8,128)(2,1)} %param.6), channel_id=1, source_target_pairs={{0,16},{8,24},{16,32},{24,40},{32,48},{40,56},{48,64},{56,72},{64,... | collective-permute-start | bytes 786440 | tf_op jit(solution)/shard_map/ppermute | solution.py:12
  33.1 6.4 %copy-start.1 = (bf16[1024,128]{1,0:T(8,128)(2,1)S(1)}, bf16[1024,128]{1,0:T(8,128)(2,1)}, u32[]{:S(2)}) copy-start(bf16[1024,128]{1,0:T(8,128)(2,1)} %param.6) | copy-start | bytes 786436
  33.1 6.4 %copy-start.2 = (bf16[128,512]{1,0:T(8,128)(2,1)S(1)}, bf16[128,512]{1,0:T(8,128)(2,1)}, u32[]{:S(2)}) copy-start(bf16[128,512]{1,0:T(8,128)(2,1)} %param.8) | copy-start | bytes 393220
  63.1 6.0 %copy-start.3 = (bf16[1024,512]{1,0:T(8,128)(2,1)S(1)}, bf16[1024,512]{1,0:T(8,128)(2,1)}, u32[]{:S(2)}) copy-start(bf16[1024,512]{1,0:T(8,128)(2,1)} %param.11) | copy-start | bytes 3145732
  63.1 6.0 %copy-start.4 = (f32[512]{0:T(512)S(1)}, f32[512]{0:T(512)}, u32[]{:S(2)}) copy-start(f32[512]{0:T(512)} %param.10) | copy-start | bytes 6148
  103.2 468.6 %collective-permute-start.4 = (bf16[1024,128]{1,0:T(8,128)(2,1)}, bf16[1024,128]{1,0:T(8,128)(2,1)S(1)}, u32[]{:S(2)}, u32[]{:S(2)}) collective-permute-start(bf16[1024,128]{1,0:T(8,128)(2,1)} %convolution_convert_fusion.3), channel_id=1, source_target_pairs={{0,760},{8,0},{16,8},{24,16},{32,24},{40,32},{48,40},{56,48},{64,5... | collective-permute-start | bytes 786440 | tf_op jit(solution)/shard_map/ppermute | solution.py:12
  107.9 463.8 %collective-permute-start.5 = (bf16[1024,128]{1,0:T(8,128)(2,1)}, bf16[1024,128]{1,0:T(8,128)(2,1)S(1)}, u32[]{:S(2)}, u32[]{:S(2)}) collective-permute-start(bf16[1024,128]{1,0:T(8,128)(2,1)} %convolution_convert_fusion.2), channel_id=1, source_target_pairs={{0,752},{8,760},{16,0},{24,8},{32,16},{40,24},{48,32},{56,40},{64,... | collective-permute-start | bytes 786440 | tf_op jit(solution)/shard_map/ppermute | solution.py:12
  110.2 461.6 %collective-permute-start.6 = (bf16[1024,128]{1,0:T(8,128)(2,1)}, bf16[1024,128]{1,0:T(8,128)(2,1)S(1)}, u32[]{:S(2)}, u32[]{:S(2)}) collective-permute-start(bf16[1024,128]{1,0:T(8,128)(2,1)} %convolution_convert_fusion.1), channel_id=1, source_target_pairs={{0,744},{8,752},{16,760},{24,0},{32,8},{40,16},{48,24},{56,32},{64... | collective-permute-start | bytes 786440 | tf_op jit(solution)/shard_map/ppermute | solution.py:12
  115.5 456.3 %collective-permute-start.7 = (bf16[1024,128]{1,0:T(8,128)(2,1)}, bf16[1024,128]{1,0:T(8,128)(2,1)S(1)}, u32[]{:S(2)}, u32[]{:S(2)}) collective-permute-start(bf16[1024,128]{1,0:T(8,128)(2,1)} %convolution_convert_fusion), channel_id=1, source_target_pairs={{0,736},{8,744},{16,752},{24,760},{32,0},{40,8},{48,16},{56,24},{6... | collective-permute-start | bytes 786440 | tf_op jit(solution)/shard_map/ppermute | solution.py:12
Sparse Core Ops, SparseCore 0:
  97.5 471.5 all-reduce.2
where the time goes:
time: 590 us; the launch traced here: 580 us
  waiting for transfers between devices  347 us (59%)
  blocking collectives  114 us (19%)
  matrix products  61 us (10%)
  starting transfers between devices  39.7 us (7%)
  between operations  14.7 us (2%)
    psum x1, waiting for transfers between devices, shards(): lax.psum((term_self, term_neigh, term_bias), ('blk', 'rep'))  336 us
    psum x1, blocking collectives, shards(): lax.psum((term_self, term_neigh, term_bias), ('blk', 'rep'))  114 us
    ppermute x8, starting transfers between devices, shifted(): lax.ppermute(array, axis, [(i, (i + by) % peers) for i in range(peers)])  39.6 us
    dot_general x5, matrix products, shards(): jnp.dot(tiles[back], blocks[back], preferred_element_type=jnp.float32)  25.3 us
    dot_general x4, matrix products, shards(): lax.dot_general(tiles[back], dmean, contract, preferred_element_type=jnp....  23.1 us
  transfers between devices with their start and end apart: 9, of which 3 were waited for; matrix products, arithmetic and copies ran while one was open for 5% of the time, Pallas kernels for 0%

commit v1 on v0

v1 whole, which is shorter than its diff:
```python
import functools

import jax
import jax.numpy as jnp
import numpy as np
from jax import lax
from jax.experimental import pallas as pl
from jax.experimental.pallas import tpu as pltpu
from jax.sharding import Mesh
from jax.sharding import PartitionSpec as P

FAN = 10
STEPS = 4
WINDOW_TILE = 256
NODE_TILE = 256
LANES = 128
SUBLANES = 8
PACK = 16
VMEM = 24 * 1024 * 1024
BF16 = jnp.bfloat16
F32 = jnp.float32

GRID = (("x", 4), ("z", 12), ("far", 2), ("near", 4), ("core", 2))
AXES = tuple(name for name, _ in GRID)
FIRST = ("x", "far", "near", "core")
SECOND = ("z",)

ROWS_FIRST = (((0,), (0,)), ((), ()))
COLS_LAST = (((1,), (1,)), ((), ()))


def dot(a, b, contract=(((1,), (0,)), ((), ()))):
    return lax.dot_general(a, b, contract, preferred_element_type=F32)


def count_kernel(near_ref, out_ref):
    row = lax.broadcasted_iota(jnp.int32, (PACK, LANES), 0)
    rows = [(row + PACK * g).astype(jnp.int16) for g in range(WINDOW_TILE // PACK)]
    one = jnp.ones((PACK, LANES), BF16)
    zero = jnp.zeros((PACK, LANES), BF16)

    @pl.loop(0, out_ref.shape[0] // WINDOW_TILE)
    def _(step):
        low = pl.multiple_of(step * WINDOW_TILE, WINDOW_TILE)
        key = (near_ref[...] - low).astype(jnp.int16)
        for lane in range(near_ref.shape[1] // LANES):
            cols = slice(lane * LANES, (lane + 1) * LANES)
            keys = [jnp.broadcast_to(key[k : k + 1, cols], (PACK, LANES)) for k in range(FAN)]
            for g in range(WINDOW_TILE // PACK):
                count = jnp.where(rows[g] == keys[0], one, zero)
                for k in range(1, FAN):
                    count = count + jnp.where(rows[g] == keys[k], one, zero)
                out_ref[pl.ds(low + g * PACK, PACK), cols] = count


def in_vmem():
    return pl.BlockSpec(memory_space=pltpu.VMEM)


def count_tiles(near):
    entries, rows = near.shape
    window = (STEPS + 1) * rows
    return pl.pallas_call(
        count_kernel,
        in_specs=[in_vmem()],
        out_specs=in_vmem(),
        out_shape=jax.ShapeDtypeStruct((window, rows), BF16),
        cost_estimate=pl.CostEstimate(
            flops=3 * entries * window * rows, bytes_accessed=2 * window * rows, transcendentals=0
        ),
        compiler_params=pltpu.CompilerParams(vmem_limit_bytes=VMEM),
        name="count_tiles",
    )(near)


def whole(array):
    return pl.BlockSpec(array.shape, lambda *_: (0,) * array.ndim)


def gather_kernel(window_blocks, tile_ref, *refs):
    *blocks, out_ref = refs
    rows = blocks[0].shape[0]
    total = None
    for back, block in zip(window_blocks, blocks):
        term = dot(block[...], tile_ref[back * rows : (back + 1) * rows, :], ROWS_FIRST)
        total = term if total is None else total + term
    out_ref[...] = total


def gather_sum(tiles, window_blocks, blocks):
    rows, width = blocks[0].shape
    steps = len(blocks)
    return pl.pallas_call(
        functools.partial(gather_kernel, window_blocks),
        in_specs=[in_vmem()] * (1 + steps),
        out_specs=in_vmem(),
        out_shape=jax.ShapeDtypeStruct((width, rows), F32),
        cost_estimate=pl.CostEstimate(
            flops=2 * steps * rows * rows * width,
            bytes_accessed=2 * steps * rows * width,
            transcendentals=0,
        ),
        compiler_params=pltpu.CompilerParams(vmem_limit_bytes=VMEM),
        name="gather_sum",
    )(tiles, *blocks)


def layer_kernel(
    back,
    chunk_rows,
    tile_ref,
    part_ref,
    block_ref,
    w_self_ref,
    w_neigh_ref,
    bias_ref,
    own_ref,
    cot_ref,
    hidden_ref,
    send_ref,
    own_part_ref,
    near_part_ref,
    far_part_ref,
    total_ref,
    grad_ref,
    gbias_ref,
    w_ref,
    dmean_ref,
):
    rows, width = block_ref.shape
    hid = w_ref.shape[1]
    step = pl.program_id(0)

    @pl.when(step == 0)
    def _():
        tile = tile_ref[back * rows : (back + 1) * rows, :]
        total_ref[...] = part_ref[...] + dot(block_ref[...], tile, ROWS_FIRST)
        grad_ref[...] = jnp.zeros_like(grad_ref)
        gbias_ref[...] = jnp.zeros_like(gbias_ref)
        w_ref[:width, :] = w_self_ref[...]
        w_ref[width:, :] = w_neigh_ref[...]

    weights = w_ref[...]
    span = pl.ds(pl.multiple_of(step * NODE_TILE, NODE_TILE), NODE_TILE)
    mean = (total_ref[:, span].T / FAN).astype(BF16)
    both = jnp.concatenate([own_ref[...], mean], axis=1)
    pre = dot(both, weights) + bias_ref[...]
    sig = jax.nn.sigmoid(pre)
    hidden_ref[...] = (pre * sig).astype(BF16)
    slope = sig * (1.0 + pre * (1.0 - sig))
    dpre = (cot_ref[...].astype(F32) * slope).astype(BF16)
    grad_ref[...] += dot(both, dpre, ROWS_FIRST)
    gbias_ref[...] += jnp.sum(dpre.astype(F32), axis=0, keepdims=True)
    back_both = dot(dpre, weights, COLS_LAST)
    own_part_ref[span, :] = back_both[:, :width]
    dmean_ref[span, :] = (back_both[:, width:] / FAN).astype(BF16)

    @pl.when(step == pl.num_programs(0) - 1)
    def _():
        pieces = hid // LANES
        spare = send_ref.shape[1] - chunk_rows - pieces
        folded = [gbias_ref[:, p * LANES : (p + 1) * LANES] for p in range(pieces)]
        folded = jnp.concatenate([*folded, jnp.zeros((spare, LANES), F32)], axis=0)
        for chunk in range(send_ref.shape[0]):
            top, left = chunk // pieces * chunk_rows, chunk % pieces * LANES
            term = grad_ref[top : top + chunk_rows, left : left + LANES]
            send_ref[chunk] = jnp.concatenate([term, folded], axis=0).astype(BF16)
        dmean = dmean_ref[...]
        for steps_back in reversed(range(STEPS + 1)):
            term = dot(tile_ref[steps_back * rows : (steps_back + 1) * rows, :], dmean)
            if steps_back == 0:
                own_part_ref[...] += term
            else:
                out_ref, at = (near_part_ref, 1) if steps_back < 3 else (far_part_ref, 3)
                first = (steps_back - at) * rows
                out_ref[first : first + rows, :] = term.astype(BF16)


def layer(tiles, part, block, back, own, w_self, w_neigh, bias, cotangent, copies):
    rows, width = own.shape
    hid = w_self.shape[1]
    chunk_rows = 2 * width * hid // (copies * LANES)
    bias_rows = -(-hid // (LANES * SUBLANES)) * SUBLANES

    def tiled(columns):
        return pl.BlockSpec((NODE_TILE, columns), lambda i: (i, 0))

    outs = (
        jax.ShapeDtypeStruct((rows, hid), BF16),
        jax.ShapeDtypeStruct((copies, chunk_rows + bias_rows, LANES), BF16),
        jax.ShapeDtypeStruct((rows, width), F32),
        jax.ShapeDtypeStruct((2 * rows, width), BF16),
        jax.ShapeDtypeStruct((2 * rows, width), BF16),
    )
    return pl.pallas_call(
        functools.partial(layer_kernel, back, chunk_rows),
        grid=(rows // NODE_TILE,),
        in_specs=[in_vmem()] * 6 + [tiled(width), tiled(hid)],
        out_specs=[tiled(hid)] + [whole(o) for o in outs[1:]],
        out_shape=outs,
        scratch_shapes=[
            pltpu.VMEM((width, rows), F32),
            pltpu.VMEM((2 * width, hid), F32),
            pltpu.VMEM((1, hid), F32),
            pltpu.VMEM((2 * width, hid), BF16),
            pltpu.VMEM((rows, width), BF16),
        ],
        cost_estimate=pl.CostEstimate(
            flops=12 * rows * rows * width + 12 * rows * width * hid,
            bytes_accessed=4 * rows * hid,
            transcendentals=2 * rows * hid,
        ),
        compiler_params=pltpu.CompilerParams(vmem_limit_bytes=VMEM),
        name="layer",
    )(tiles, part, block, w_self, w_neigh, bias, own, cotangent)


def unfold_kernel(chunks_ref, *out_refs):
    rows, columns = out_refs[0].shape
    copies, chunk_rows, lanes = chunks_ref.shape
    pieces = columns // lanes
    for chunk in range(copies):
        top, left = chunk // pieces * chunk_rows, chunk % pieces * lanes
        out_ref, top = out_refs[top // rows], top % rows
        out_ref[top : top + chunk_rows, left : left + lanes] = chunks_ref[chunk].astype(F32)


def unfold(chunks, rows, columns):
    return pl.pallas_call(
        unfold_kernel,
        out_shape=[jax.ShapeDtypeStruct((rows, columns), F32)] * 2,
        compiler_params=pltpu.CompilerParams(vmem_limit_bytes=VMEM),
        name="unfold",
    )(chunks)


def shift_pairs(by):
    sizes = [n for _, n in GRID]
    group = sizes[3] * sizes[4]
    peers = sizes[0] * sizes[1] * sizes[2]
    return [
        (b * group + r, ((b + by) % peers) * group + r) for b in range(peers) for r in range(group)
    ]


def shifted(array, by):
    return lax.ppermute(array, AXES, shift_pairs(by))


def exchange(array, axes):
    return lax.all_to_all(array, axes, 0, 0, tiled=True)


def sum_parts(array):
    return jnp.sum(array.astype(F32), axis=0)


def to_all(array, axes):
    return exchange(jnp.broadcast_to(array[None], (lax.axis_size(axes),) + array.shape), axes)


def shards(features, neighbours, w_self, w_neigh, bias, cotangent):
    rows, width = features.shape
    hid = w_self.shape[1]
    n_first = lax.axis_size(FIRST)
    near1 = shifted(features, 1)
    near2 = shifted(features, 2)
    near4 = shifted(features, 4)
    tiles = count_tiles(neighbours.T)
    near1, tiles = lax.optimization_barrier((near1, tiles))
    near3 = shifted(near1, 2)
    part = gather_sum(tiles, (0, 2, 4, 1), (features, near2, near4, near1))
    hidden, send, own, near, far = layer(
        tiles, part, near3, 3, features, w_self, w_neigh, bias[None], cotangent, n_first
    )
    far = shifted(far, -2)
    chunk = sum_parts(exchange(send, FIRST)).astype(BF16)
    far, _ = lax.optimization_barrier((far, chunk))
    near = near.astype(F32) + far.astype(F32)
    got1 = shifted(near[:rows].astype(BF16), -1)
    got2 = shifted(near[rows:].astype(BF16), -2)

    scale = 1.0 / (rows * lax.axis_size(AXES)) ** 0.5
    total = sum_parts(to_all(chunk, SECOND)) * scale
    pieces = hid // LANES
    chunk_rows = 2 * width * pieces // n_first
    grads = unfold(to_all(total[:chunk_rows].astype(BF16), FIRST), width, hid)
    g_bias = total[chunk_rows : chunk_rows + pieces].reshape(hid)
    grad_x = own + got1.astype(F32) + got2.astype(F32)
    return hidden, grad_x.astype(BF16), *grads, g_bias


def solution(mesh):
    grid = Mesh(mesh.devices.reshape([n for _, n in GRID]), AXES)
    node = P(AXES, None)
    return jax.shard_map(
        shards,
        mesh=grid,
        in_specs=(node, node, P(), P(), P(), node),
        out_specs=(node, node, P(), P(), P()),
        check_vma=False,
    )
```

time: 590 us -> 120 us (0.20); the launches traced: 580 us -> 119 us
  waiting for transfers between devices: 347 us -> 30.9 us
  blocking collectives: 114 us -> 0 us
  matrix products: 61 us -> 0 us
  starting transfers between devices: 39.7 us -> 62.6 us
  Pallas kernels: 0 us -> 20.7 us
  between operations: 14.7 us -> 0.83 us
    psum x1 -> x0, waiting for transfers between devices: 336 us -> none  [shards(): lax.psum((term_self, term_neigh, term_bias), ('blk', 'rep'))]
    psum x1 -> x0, blocking collectives: 114 us -> none  [shards(): lax.psum((term_self, term_neigh, term_bias), ('blk', 'rep'))]
    dot_general x16 -> x0, matrix products: 61 us -> none  [the longest x5 25.3 us: shards(): jnp.dot(tiles[back], blocks[back], preferred_element_type=jnp.float32)]
    all_to_all x0 -> x3, starting transfers between devices: none -> 22 us  [exchange(): return lax.all_to_all(array, axes, 0, 0, tiled=True)]
    pallas_call x0 -> x4, Pallas kernels: none -> 20.7 us  [the longest x1 11.7 us: count_tiles(): pl.pallas_call(count_kernel, in_specs=[in_vmem()], out_specs=in_vmem(), o...]
    all_to_all x0 -> x3, waiting for transfers between devices: none -> 16.2 us  [exchange(): return lax.all_to_all(array, axes, 0, 0, tiled=True)]
    ppermute x8 -> x7, waiting for transfers between devices: 10.1 us -> 14.7 us  [shifted(): return lax.ppermute(array, AXES, shift_pairs(by))]
    ppermute x8 -> x7, starting transfers between devices: 39.6 us -> 40.6 us  [shifted(): return lax.ppermute(array, AXES, shift_pairs(by))]
  transfers between devices with their start and end apart: 9 -> 10, of which waited for: 3 -> 6; matrix products, arithmetic and copies ran while one was open for 5% -> 3% of each run, Pallas kernels for 0% -> 11%
where the time goes in v1:
time: 120 us; the launch traced here: 119 us
  starting transfers between devices  62.6 us (52%)
  waiting for transfers between devices  30.9 us (26%)
  Pallas kernels  20.7 us (17%)
  local copies, waits for them, and re-layouts  2.86 us (2%)
    ppermute x7, starting transfers between devices, shifted(): return lax.ppermute(array, AXES, shift_pairs(by))  40.6 us
    all_to_all x3, starting transfers between devices, exchange(): return lax.all_to_all(array, axes, 0, 0, tiled=True)  22 us
    all_to_all x3, waiting for transfers between devices, exchange(): return lax.all_to_all(array, axes, 0, 0, tiled=True)  16.2 us
    ppermute x7, waiting for transfers between devices, shifted(): return lax.ppermute(array, AXES, shift_pairs(by))  14.7 us
    pallas_call x1, Pallas kernels, count_tiles(): pl.pallas_call(count_kernel, in_specs=[in_vmem()], out_specs=in_vmem(), o...  11.7 us
    pallas_call x1, Pallas kernels, layer(): pl.pallas_call(functools.partial(layer_kernel, back, chunk_rows), grid=(r...  6.94 us
  transfers between devices with their start and end apart: 10, of which 6 were waited for; matrix products, arithmetic and copies ran while one was open for 3% of the time, Pallas kernels for 11%

profile of v1, /device:TPU:1, one launch (start us, length us, event | category | flops | bytes accessed | tf_op | source)
XLA Modules:
  0.0 119.0 jit_solution(3605114804256466552)
XLA Ops:
  0.6 8.4 %collective-permute-start = (bf16[1024,128]{1,0:T(8,128)(2,1)}, bf16[1024,128]{1,0:T(8,128)(2,1)S(1)}, u32[]{:S(2)}, u32[]{:S(2)}) collective-permute-start(bf16[1024,128]{1,0:T(8,128)(2,1)} %own_ref.1), channel_id=1, source_target_pairs={{0,8},{1,9},{2,10},{3,11},{4,12},{5,13},{6,14},{7,15},{8,16},{9,17... | collective-permute-start | bytes 786440 | tf_op jit(solution)/shard_map/ppermute | solution.py:247
  9.1 5.8 %collective-permute-start.2 = (bf16[1024,128]{1,0:T(8,128)(2,1)}, bf16[1024,128]{1,0:T(8,128)(2,1)S(1)}, u32[]{:S(2)}, u32[]{:S(2)}) collective-permute-start(bf16[1024,128]{1,0:T(8,128)(2,1)} %own_ref.1), channel_id=1, source_target_pairs={{0,32},{1,33},{2,34},{3,35},{4,36},{5,37},{6,38},{7,39},{8,40},{9,... | collective-permute-start | bytes 786440 | tf_op jit(solution)/shard_map/ppermute | solution.py:247
  14.9 4.0 %collective-permute-start.1 = (bf16[1024,128]{1,0:T(8,128)(2,1)}, bf16[1024,128]{1,0:T(8,128)(2,1)S(1)}, u32[]{:S(2)}, u32[]{:S(2)}) collective-permute-start(bf16[1024,128]{1,0:T(8,128)(2,1)} %own_ref.1), channel_id=1, source_target_pairs={{0,16},{1,17},{2,18},{3,19},{4,20},{5,21},{6,22},{7,23},{8,24},{9,... | collective-permute-start | bytes 786440 | tf_op jit(solution)/shard_map/ppermute | solution.py:247
  18.9 0.8 copy-done.4
  19.7 11.7 %count_tiles.1.tile_ref = bf16[5120,1024]{1,0:T(8,128)(2,1)S(1)} custom-call(s32[10,1024]{1,0:T(8,128)S(1)} %bitcast.4), custom_call_target="tpu_custom_call" | custom-call | flops 157286400 | bytes 10485760 | tf_op jit(solution)/shard_map/count_tiles/pallas_call | solution.py:63
  31.4 3.6 %collective-permute-done.refs_3_ = bf16[1024,128]{1,0:T(8,128)(2,1)S(1)} collective-permute-done((bf16[1024,128]{1,0:T(8,128)(2,1)}, bf16[1024,128]{1,0:T(8,128)(2,1)S(1)}, u32[]{:S(2)}, u32[]{:S(2)}) %collective-permute-start) | collective-permute-done | bytes 262176 | tf_op jit(solution)/shard_map/ppermute | solution.py:247
  35.1 1.9 %collective-permute-start.3 = (bf16[1024,128]{1,0:T(8,128)(2,1)S(1)}, bf16[1024,128]{1,0:T(8,128)(2,1)S(1)}, u32[]{:S(2)}, u32[]{:S(2)}) collective-permute-start(bf16[1024,128]{1,0:T(8,128)(2,1)S(1)} %collective-permute-done.refs_3_), channel_id=1, source_target_pairs={{0,16},{1,17},{2,18},{3,19},{4,20},{5,21},{6,22},{7,23},{8,24},{9,... | collective-permute-start | bytes 786440 | tf_op jit(solution)/shard_map/ppermute | solution.py:247
  37.0 0.0 collective-permute-done.2.refs_2_
  37.0 6.7 %collective-permute-done.1.refs_1_ = bf16[1024,128]{1,0:T(8,128)(2,1)S(1)} collective-permute-done((bf16[1024,128]{1,0:T(8,128)(2,1)}, bf16[1024,128]{1,0:T(8,128)(2,1)S(1)}, u32[]{:S(2)}, u32[]{:S(2)}) %collective-permute-start.1) | collective-permute-done | bytes 262176 | tf_op jit(solution)/shard_map/ppermute | solution.py:247
  43.8 1.3 %gather_sum.1.part_ref = f32[128,1024]{1,0:T(8,128)S(1)} custom-call(bf16[5120,1024]{1,0:T(8,128)(2,1)S(1)} %count_tiles.1.tile_ref, bf16[1024,128]{1,0:T(8,128)(2,1)S(1)} %copy-done, bf16[1024,128]{1,0:T(8,128)(2,1)S(1)} %collective-permute-done.1.refs_1_, bf16[1024,128]{1,0:T(8,128)(2,1)S(1)} %collective-permute-done.2.refs_2_, ...), custom_call_target="tpu_custom_call" | custom-call | flops 1073741824 | bytes 1048576 | tf_op jit(solution)/shard_map/gather_sum/pallas_call | solution.py:93
  45.1 3.0 %collective-permute-done.3.block_ref = bf16[1024,128]{1,0:T(8,128)(2,1)S(1)} collective-permute-done((bf16[1024,128]{1,0:T(8,128)(2,1)S(1)}, bf16[1024,128]{1,0:T(8,128)(2,1)S(1)}, u32[]{:S(2)}, u32[]{:S(2)}) %collective-permute-start.3) | collective-permute-done | bytes 262176 | tf_op jit(solution)/shard_map/ppermute | solution.py:247
  48.1 0.0 copy-done.1
  48.1 6.9 %layer.1 = (bf16[1024,512]{1,0:T(8,128)(2,1)}, bf16[64,24,128]{2,1,0:T(8,128)(2,1)}, f32[1024,128]{1,0:T(8,128)S(1)}, bf16[2048,128]{1,0:T(8,128)(2,1)S(1)}, bf16[2048,128]{1,0:T(8,128)(2,1)S(1)}) custom-call(bf16[5120,1024]{1,0:T(8,128)(2,1)S(1)} %count_tiles.1.tile_ref, f32[128,1024]{1,0:T(8,128)S(1)} %gather_sum.1.part_ref, ...), custom_call_target="tpu_custom_call" | custom-call | flops 2415919104 | bytes 2097152 | tf_op jit(solution)/shard_map/layer/pallas_call | solution.py:195
  55.1 10.1 %all-to-all-start = ((bf16[64,24,128]{2,1,0:T(8,128)(2,1)}), bf16[64,24,128]{2,1,0:T(8,128)(2,1)S(1)}, u32[]{:S(2)}, u32[]{:S(2)}) async-start(bf16[64,24,128]{2,1,0:T(8,128)(2,1)} %get-tuple-element.21), calls=%async_computation | async-start | bytes 786432 | tf_op jit(solution)/shard_map/all_to_all | solution.py:251
  65.2 7.8 %collective-permute-start.4 = (bf16[2048,128]{1,0:T(8,128)(2,1)S(1)}, bf16[2048,128]{1,0:T(8,128)(2,1)S(1)}, u32[]{:S(2)}, u32[]{:S(2)}) collective-permute-start(bf16[2048,128]{1,0:T(8,128)(2,1)S(1)} %get-tuple-element.20), channel_id=1, source_target_pairs={{0,752},{1,753},{2,754},{3,755},{4,756},{5,757},{6,758},{7,759},{8... | collective-permute-start | bytes 1572872 | tf_op jit(solution)/shard_map/ppermute | solution.py:247
  73.0 6.8 %all-to-all-done = bf16[64,24,128]{2,1,0:T(8,128)(2,1)S(1)} async-done(((bf16[64,24,128]{2,1,0:T(8,128)(2,1)}), bf16[64,24,128]{2,1,0:T(8,128)(2,1)S(1)}, u32[]{:S(2)}, u32[]{:S(2)}) %all-to-all-start) | async-done | bytes 393248 | tf_op jit(solution)/shard_map/all_to_all | solution.py:251
  79.8 0.1 reduce_sum.21
  79.9 0.6 broadcast_in_dim.7
  80.6 5.7 %all-to-all-start.1 = ((bf16[12,24,128]{2,1,0:T(8,128)(2,1)}), bf16[12,24,128]{2,1,0:T(8,128)(2,1)S(1)}, u32[]{:S(2)}, u32[]{:S(2)}) async-start(bf16[12,24,128]{2,1,0:T(8,128)(2,1)} %broadcast_in_dim.7), calls=%async_computation.1 | async-start | bytes 147456 | tf_op jit(solution)/shard_map/all_to_all | solution.py:251
  86.3 0.0 collective-permute-done.4
  86.3 0.1 add_convert_fusion
  86.5 10.8 %collective-permute-start.5 = (bf16[1024,128]{1,0:T(8,128)(2,1)S(1)}, bf16[1024,128]{1,0:T(8,128)(2,1)S(1)}, u32[]{:S(2)}, u32[]{:S(2)}) collective-permute-start(bf16[1024,128]{1,0:T(8,128)(2,1)S(1)} %get-tuple-element.25), channel_id=1, source_target_pairs={{0,760},{1,761},{2,762},{3,763},{4,764},{5,765},{6,766},{7,767},{8... | collective-permute-start | bytes 786440 | tf_op jit(solution)/shard_map/ppermute | solution.py:247
  97.2 1.9 %collective-permute-start.6 = (bf16[1024,128]{1,0:T(8,128)(2,1)S(1)}, bf16[1024,128]{1,0:T(8,128)(2,1)S(1)}, u32[]{:S(2)}, u32[]{:S(2)}) collective-permute-start(bf16[1024,128]{1,0:T(8,128)(2,1)S(1)} %get-tuple-element.26), channel_id=1, source_target_pairs={{0,752},{1,753},{2,754},{3,755},{4,756},{5,757},{6,758},{7,759},{8... | collective-permute-start | bytes 786440 | tf_op jit(solution)/shard_map/ppermute | solution.py:247
  99.2 0.0 all-to-all-done.1
  99.2 0.7 broadcast_in_dim.8
  100.0 6.2 %all-to-all-start.2 = ((bf16[64,16,128]{2,1,0:T(8,128)(2,1)}), bf16[64,16,128]{2,1,0:T(8,128)(2,1)S(1)}, u32[]{:S(2)}, u32[]{:S(2)}) async-start(bf16[64,16,128]{2,1,0:T(8,128)(2,1)} %broadcast_in_dim.8), calls=%async_computation.2 | async-start | bytes 524288 | tf_op jit(solution)/shard_map/all_to_all | solution.py:251
  106.1 0.6 slice_bitcast_fusion
  106.7 0.0 collective-permute-done.5
  106.7 1.2 %collective-permute-done.6 = bf16[1024,128]{1,0:T(8,128)(2,1)S(1)} collective-permute-done((bf16[1024,128]{1,0:T(8,128)(2,1)S(1)}, bf16[1024,128]{1,0:T(8,128)(2,1)S(1)}, u32[]{:S(2)}, u32[]{:S(2)}) %collective-permute-start.6) | collective-permute-done | bytes 262176 | tf_op jit(solution)/shard_map/ppermute | solution.py:247
  107.9 0.8 add_convert_fusion.1
  108.7 9.4 %all-to-all-done.2.chunks_ref = bf16[64,16,128]{2,1,0:T(8,128)(2,1)S(1)} async-done(((bf16[64,16,128]{2,1,0:T(8,128)(2,1)}), bf16[64,16,128]{2,1,0:T(8,128)(2,1)S(1)}, u32[]{:S(2)}, u32[]{:S(2)}) %all-to-all-start.2) | async-done | bytes 262176 | tf_op jit(solution)/shard_map/all_to_all | solution.py:251
  118.2 0.8 unfold.1
  (14 shorter events, 0.1 us)
Async XLA Ops:
  0.6 43.1 %copy-start = (bf16[1024,128]{1,0:T(8,128)(2,1)S(1)}, bf16[1024,128]{1,0:T(8,128)(2,1)}, u32[]{:S(2)}) copy-start(bf16[1024,128]{1,0:T(8,128)(2,1)} %own_ref.1) | copy-start | bytes 786436
  0.6 34.4 %collective-permute-start = (bf16[1024,128]{1,0:T(8,128)(2,1)}, bf16[1024,128]{1,0:T(8,128)(2,1)S(1)}, u32[]{:S(2)}, u32[]{:S(2)}) collective-permute-start(bf16[1024,128]{1,0:T(8,128)(2,1)} %own_ref.1), channel_id=1, source_target_pairs={{0,8},{1,9},{2,10},{3,11},{4,12},{5,13},{6,14},{7,15},{8,16},{9,17... | collective-permute-start | bytes 786440 | tf_op jit(solution)/shard_map/ppermute | solution.py:247
  9.1 27.9 %collective-permute-start.2 = (bf16[1024,128]{1,0:T(8,128)(2,1)}, bf16[1024,128]{1,0:T(8,128)(2,1)S(1)}, u32[]{:S(2)}, u32[]{:S(2)}) collective-permute-start(bf16[1024,128]{1,0:T(8,128)(2,1)} %own_ref.1), channel_id=1, source_target_pairs={{0,32},{1,33},{2,34},{3,35},{4,36},{5,37},{6,38},{7,39},{8,40},{9,... | collective-permute-start | bytes 786440 | tf_op jit(solution)/shard_map/ppermute | solution.py:247
  14.9 28.9 %collective-permute-start.1 = (bf16[1024,128]{1,0:T(8,128)(2,1)}, bf16[1024,128]{1,0:T(8,128)(2,1)S(1)}, u32[]{:S(2)}, u32[]{:S(2)}) collective-permute-start(bf16[1024,128]{1,0:T(8,128)(2,1)} %own_ref.1), channel_id=1, source_target_pairs={{0,16},{1,17},{2,18},{3,19},{4,20},{5,21},{6,22},{7,23},{8,24},{9,... | collective-permute-start | bytes 786440 | tf_op jit(solution)/shard_map/ppermute | solution.py:247
  18.9 0.8 copy-start.4
  19.7 28.4 %copy-start.1 = (bf16[1024,512]{1,0:T(8,128)(2,1)S(1)}, bf16[1024,512]{1,0:T(8,128)(2,1)}, u32[]{:S(2)}) copy-start(bf16[1024,512]{1,0:T(8,128)(2,1)} %cot_ref.1) | copy-start | bytes 3145732
  19.7 28.4 %copy-start.2 = (bf16[128,512]{1,0:T(8,128)(2,1)S(1)}, bf16[128,512]{1,0:T(8,128)(2,1)}, u32[]{:S(2)}) copy-start(bf16[128,512]{1,0:T(8,128)(2,1)} %w_self_ref.1) | copy-start | bytes 393220
  19.7 28.4 %copy-start.3 = (bf16[128,512]{1,0:T(8,128)(2,1)S(1)}, bf16[128,512]{1,0:T(8,128)(2,1)}, u32[]{:S(2)}) copy-start(bf16[128,512]{1,0:T(8,128)(2,1)} %w_neigh_ref.1) | copy-start | bytes 393220
  19.7 28.4 %copy-start.5 = (f32[512]{0:T(512)S(1)}, f32[512]{0:T(512)}, u32[]{:S(2)}) copy-start(f32[512]{0:T(512)} %param.10) | copy-start | bytes 6148
  35.1 13.0 %collective-permute-start.3 = (bf16[1024,128]{1,0:T(8,128)(2,1)S(1)}, bf16[1024,128]{1,0:T(8,128)(2,1)S(1)}, u32[]{:S(2)}, u32[]{:S(2)}) collective-permute-start(bf16[1024,128]{1,0:T(8,128)(2,1)S(1)} %collective-permute-done.refs_3_), channel_id=1, source_target_pairs={{0,16},{1,17},{2,18},{3,19},{4,20},{5,21},{6,22},{7,23},{8,24},{9,... | collective-permute-start | bytes 786440 | tf_op jit(solution)/shard_map/ppermute | solution.py:247
  55.1 24.7 %all-to-all-start = ((bf16[64,24,128]{2,1,0:T(8,128)(2,1)}), bf16[64,24,128]{2,1,0:T(8,128)(2,1)S(1)}, u32[]{:S(2)}, u32[]{:S(2)}) async-start(bf16[64,24,128]{2,1,0:T(8,128)(2,1)} %get-tuple-element.21), calls=%async_computation | async-start | bytes 786432 | tf_op jit(solution)/shard_map/all_to_all | solution.py:251
  65.2 21.1 %collective-permute-start.4 = (bf16[2048,128]{1,0:T(8,128)(2,1)S(1)}, bf16[2048,128]{1,0:T(8,128)(2,1)S(1)}, u32[]{:S(2)}, u32[]{:S(2)}) collective-permute-start(bf16[2048,128]{1,0:T(8,128)(2,1)S(1)} %get-tuple-element.20), channel_id=1, source_target_pairs={{0,752},{1,753},{2,754},{3,755},{4,756},{5,757},{6,758},{7,759},{8... | collective-permute-start | bytes 1572872 | tf_op jit(solution)/shard_map/ppermute | solution.py:247
  80.6 18.6 %all-to-all-start.1 = ((bf16[12,24,128]{2,1,0:T(8,128)(2,1)}), bf16[12,24,128]{2,1,0:T(8,128)(2,1)S(1)}, u32[]{:S(2)}, u32[]{:S(2)}) async-start(bf16[12,24,128]{2,1,0:T(8,128)(2,1)} %broadcast_in_dim.7), calls=%async_computation.1 | async-start | bytes 147456 | tf_op jit(solution)/shard_map/all_to_all | solution.py:251
  86.5 20.3 %collective-permute-start.5 = (bf16[1024,128]{1,0:T(8,128)(2,1)S(1)}, bf16[1024,128]{1,0:T(8,128)(2,1)S(1)}, u32[]{:S(2)}, u32[]{:S(2)}) collective-permute-start(bf16[1024,128]{1,0:T(8,128)(2,1)S(1)} %get-tuple-element.25), channel_id=1, source_target_pairs={{0,760},{1,761},{2,762},{3,763},{4,764},{5,765},{6,766},{7,767},{8... | collective-permute-start | bytes 786440 | tf_op jit(solution)/shard_map/ppermute | solution.py:247
  97.2 10.7 %collective-permute-start.6 = (bf16[1024,128]{1,0:T(8,128)(2,1)S(1)}, bf16[1024,128]{1,0:T(8,128)(2,1)S(1)}, u32[]{:S(2)}, u32[]{:S(2)}) collective-permute-start(bf16[1024,128]{1,0:T(8,128)(2,1)S(1)} %get-tuple-element.26), channel_id=1, source_target_pairs={{0,752},{1,753},{2,754},{3,755},{4,756},{5,757},{6,758},{7,759},{8... | collective-permute-start | bytes 786440 | tf_op jit(solution)/shard_map/ppermute | solution.py:247
  100.0 18.2 %all-to-all-start.2 = ((bf16[64,16,128]{2,1,0:T(8,128)(2,1)}), bf16[64,16,128]{2,1,0:T(8,128)(2,1)S(1)}, u32[]{:S(2)}, u32[]{:S(2)}) async-start(bf16[64,16,128]{2,1,0:T(8,128)(2,1)} %broadcast_in_dim.8), calls=%async_computation.2 | async-start | bytes 524288 | tf_op jit(solution)/shard_map/all_to_all | solution.py:251

commit v2 on v1

--- a/solution.py
+++ b/solution.py
@@ -11,6 +11,7 @@
 
 FAN = 10
 STEPS = 4
+CLOSE = 3
 WINDOW_TILE = 256
 NODE_TILE = 256
 LANES = 128
@@ -33,7 +34,7 @@
     return lax.dot_general(a, b, contract, preferred_element_type=F32)
 
 
-def count_kernel(near_ref, out_ref):
+def count_kernel(first, near_ref, out_ref):
     row = lax.broadcasted_iota(jnp.int32, (PACK, LANES), 0)
     rows = [(row + PACK * g).astype(jnp.int16) for g in range(WINDOW_TILE // PACK)]
     one = jnp.ones((PACK, LANES), BF16)
@@ -42,7 +43,7 @@
     @pl.loop(0, out_ref.shape[0] // WINDOW_TILE)
     def _(step):
         low = pl.multiple_of(step * WINDOW_TILE, WINDOW_TILE)
-        key = (near_ref[...] - low).astype(jnp.int16)
+        key = (near_ref[...] - (first + low)).astype(jnp.int16)
         for lane in range(near_ref.shape[1] // LANES):
             cols = slice(lane * LANES, (lane + 1) * LANES)
             keys = [jnp.broadcast_to(key[k : k + 1, cols], (PACK, LANES)) for k in range(FAN)]
@@ -57,11 +58,11 @@
     return pl.BlockSpec(memory_space=pltpu.VMEM)
 
 
-def count_tiles(near):
+def count_tiles(near, first, blocks):
     entries, rows = near.shape
-    window = (STEPS + 1) * rows
-    return pl.pallas_call(
-        count_kernel,
+    window = blocks * rows
+    return pl.pallas_call(
+        functools.partial(count_kernel, first * rows),
         in_specs=[in_vmem()],
         out_specs=in_vmem(),
         out_shape=jax.ShapeDtypeStruct((window, rows), BF16),
@@ -77,12 +78,17 @@
     return pl.BlockSpec(array.shape, lambda *_: (0,) * array.ndim)
 
 
-def gather_kernel(window_blocks, tile_ref, *refs):
+def tile_of(back, close_ref, far_ref):
+    rows = close_ref.shape[1]
+    ref, first = (close_ref, 0) if back < CLOSE else (far_ref, CLOSE)
+    return ref[(back - first) * rows : (back - first + 1) * rows, :]
+
+
+def gather_kernel(window_blocks, close_ref, far_ref, *refs):
     *blocks, out_ref = refs
-    rows = blocks[0].shape[0]
     total = None
     for back, block in zip(window_blocks, blocks):
-        term = dot(block[...], tile_ref[back * rows : (back + 1) * rows, :], ROWS_FIRST)
+        term = dot(block[...], tile_of(back, close_ref, far_ref), ROWS_FIRST)
         total = term if total is None else total + term
     out_ref[...] = total
 
@@ -92,7 +98,7 @@
     steps = len(blocks)
     return pl.pallas_call(
         functools.partial(gather_kernel, window_blocks),
-        in_specs=[in_vmem()] * (1 + steps),
+        in_specs=[in_vmem()] * (2 + steps),
         out_specs=in_vmem(),
         out_shape=jax.ShapeDtypeStruct((width, rows), F32),
         cost_estimate=pl.CostEstimate(
@@ -102,13 +108,14 @@
         ),
         compiler_params=pltpu.CompilerParams(vmem_limit_bytes=VMEM),
         name="gather_sum",
-    )(tiles, *blocks)
+    )(*tiles, *blocks)
 
 
 def layer_kernel(
     back,
     chunk_rows,
-    tile_ref,
+    close_ref,
+    far_ref,
     part_ref,
     block_ref,
     w_self_ref,
@@ -118,14 +125,13 @@
     cot_ref,
     hidden_ref,
     send_ref,
-    own_part_ref,
-    near_part_ref,
+    dself_ref,
+    dmean_ref,
     far_part_ref,
     total_ref,
     grad_ref,
     gbias_ref,
     w_ref,
-    dmean_ref,
 ):
     rows, width = block_ref.shape
     hid = w_ref.shape[1]
@@ -133,7 +139,7 @@
 
     @pl.when(step == 0)
     def _():
-        tile = tile_ref[back * rows : (back + 1) * rows, :]
+        tile = tile_of(back, close_ref, far_ref)
         total_ref[...] = part_ref[...] + dot(block_ref[...], tile, ROWS_FIRST)
         grad_ref[...] = jnp.zeros_like(grad_ref)
         gbias_ref[...] = jnp.zeros_like(gbias_ref)
@@ -152,7 +158,7 @@
     grad_ref[...] += dot(both, dpre, ROWS_FIRST)
     gbias_ref[...] += jnp.sum(dpre.astype(F32), axis=0, keepdims=True)
     back_both = dot(dpre, weights, COLS_LAST)
-    own_part_ref[span, :] = back_both[:, :width]
+    dself_ref[span, :] = back_both[:, :width]
     dmean_ref[span, :] = (back_both[:, width:] / FAN).astype(BF16)
 
     @pl.when(step == pl.num_programs(0) - 1)
@@ -165,15 +171,8 @@
             top, left = chunk // pieces * chunk_rows, chunk % pieces * LANES
             term = grad_ref[top : top + chunk_rows, left : left + LANES]
             send_ref[chunk] = jnp.concatenate([term, folded], axis=0).astype(BF16)
-        dmean = dmean_ref[...]
-        for steps_back in reversed(range(STEPS + 1)):
-            term = dot(tile_ref[steps_back * rows : (steps_back + 1) * rows, :], dmean)
-            if steps_back == 0:
-                own_part_ref[...] += term
-            else:
-                out_ref, at = (near_part_ref, 1) if steps_back < 3 else (far_part_ref, 3)
-                first = (steps_back - at) * rows
-                out_ref[first : first + rows, :] = term.astype(BF16)
+        out = dot(far_ref[...], dmean_ref[...])
+        far_part_ref[...] = out.astype(BF16)
 
 
 def layer(tiles, part, block, back, own, w_self, w_neigh, bias, cotangent, copies):
@@ -189,13 +188,13 @@
         jax.ShapeDtypeStruct((rows, hid), BF16),
         jax.ShapeDtypeStruct((copies, chunk_rows + bias_rows, LANES), BF16),
         jax.ShapeDtypeStruct((rows, width), F32),
-        jax.ShapeDtypeStruct((2 * rows, width), BF16),
-        jax.ShapeDtypeStruct((2 * rows, width), BF16),
+        jax.ShapeDtypeStruct((rows, width), BF16),
+        jax.ShapeDtypeStruct(((STEPS + 1 - CLOSE) * rows, width), BF16),
     )
     return pl.pallas_call(
         functools.partial(layer_kernel, back, chunk_rows),
         grid=(rows // NODE_TILE,),
-        in_specs=[in_vmem()] * 6 + [tiled(width), tiled(hid)],
+        in_specs=[in_vmem()] * 7 + [tiled(width), tiled(hid)],
         out_specs=[tiled(hid)] + [whole(o) for o in outs[1:]],
         out_shape=outs,
         scratch_shapes=[
@@ -203,16 +202,42 @@
             pltpu.VMEM((2 * width, hid), F32),
             pltpu.VMEM((1, hid), F32),
             pltpu.VMEM((2 * width, hid), BF16),
-            pltpu.VMEM((rows, width), BF16),
         ],
         cost_estimate=pl.CostEstimate(
-            flops=12 * rows * rows * width + 12 * rows * width * hid,
+            flops=6 * rows * rows * width + 12 * rows * width * hid,
             bytes_accessed=4 * rows * hid,
             transcendentals=2 * rows * hid,
         ),
         compiler_params=pltpu.CompilerParams(vmem_limit_bytes=VMEM),
         name="layer",
-    )(tiles, part, block, w_self, w_neigh, bias, own, cotangent)
+    )(*tiles, part, block, w_self, w_neigh, bias, own, cotangent)
+
+
+def spread_kernel(close_ref, dmean_ref, dself_ref, own_ref, near_ref):
+    rows = dmean_ref.shape[0]
+    dmean = dmean_ref[...]
+    own_ref[...] = dself_ref[...] + dot(close_ref[:rows, :], dmean)
+    near_ref[...] = dot(close_ref[rows:, :], dmean).astype(BF16)
+
+
+def spread(tiles, dmean, dself):
+    rows, width = dmean.shape
+    return pl.pallas_call(
+        spread_kernel,
+        in_specs=[in_vmem()] * 3,
+        out_specs=[in_vmem()] * 2,
+        out_shape=(
+            jax.ShapeDtypeStruct((rows, width), F32),
+            jax.ShapeDtypeStruct(((CLOSE - 1) * rows, width), BF16),
+        ),
+        cost_estimate=pl.CostEstimate(
+            flops=2 * CLOSE * rows * rows * width,
+            bytes_accessed=2 * CLOSE * rows * width,
+            transcendentals=0,
+        ),
+        compiler_params=pltpu.CompilerParams(vmem_limit_bytes=VMEM),
+        name="spread",
+    )(tiles[0], dmean, dself)
 
 
 def unfold_kernel(chunks_ref, *out_refs):
@@ -266,14 +291,17 @@
     near1 = shifted(features, 1)
     near2 = shifted(features, 2)
     near4 = shifted(features, 4)
-    tiles = count_tiles(neighbours.T)
-    near1, tiles = lax.optimization_barrier((near1, tiles))
+    entries = neighbours.T
+    tiles = count_tiles(entries, 0, CLOSE)
+    near1, tiles, entries = lax.optimization_barrier((near1, tiles, entries))
+    tiles = (tiles, count_tiles(entries, CLOSE, STEPS + 1 - CLOSE))
     near3 = shifted(near1, 2)
     part = gather_sum(tiles, (0, 2, 4, 1), (features, near2, near4, near1))
-    hidden, send, own, near, far = layer(
+    hidden, send, dself, dmean, far = layer(
         tiles, part, near3, 3, features, w_self, w_neigh, bias[None], cotangent, n_first
     )
     far = shifted(far, -2)
+    own, near = spread(tiles, dmean, dself)
     chunk = sum_parts(exchange(send, FIRST)).astype(BF16)
     far, _ = lax.optimization_barrier((far, chunk))
     near = near.astype(F32) + far.astype(F32)

time: 120 us -> 118 us (0.983)
  waiting for transfers between devices: 30.9 us -> 26.3 us
  local copies, waits for them, and re-layouts: 2.86 us -> 5.65 us
    all_to_all x3, waiting for transfers between devices: 16.2 us -> 11.7 us  [exchange(): return lax.all_to_all(array, axes, 0, 0, tiled=True)]
    unnamed x12 -> x16, local copies, waits for them, and re-layouts: 0.85 us -> 3.64 us
    pallas_call x1 -> x3, Pallas kernels: 11.7 us -> 13.5 us  [the longest x2 11.7 us: count_tiles(): pl.pallas_call(functools.partial(count_kernel, first * rows), in_specs=[i...]
    pallas_call x1, Pallas kernels: 6.94 us -> 5.3 us  [layer(): pl.pallas_call(functools.partial(layer_kernel, back, chunk_rows), grid=(r...]
  transfers between devices with their start and end apart: 10 -> 10, of which waited for: 6 -> 6; matrix products, arithmetic and copies ran while one was open for 3% -> 3% of each run, Pallas kernels for 11% -> 13%
where the time goes in v2:
time: 118 us; the launch traced here: 117 us
  starting transfers between devices  62.6 us (53%)
  waiting for transfers between devices  26.3 us (22%)
  Pallas kernels  20.9 us (18%)
  local copies, waits for them, and re-layouts  5.65 us (5%)
    ppermute x7, starting transfers between devices, shifted(): return lax.ppermute(array, AXES, shift_pairs(by))  40.6 us
    all_to_all x3, starting transfers between devices, exchange(): return lax.all_to_all(array, axes, 0, 0, tiled=True)  22 us
    ppermute x7, waiting for transfers between devices, shifted(): return lax.ppermute(array, AXES, shift_pairs(by))  14.6 us
    pallas_call x2, Pallas kernels, count_tiles(): pl.pallas_call(functools.partial(count_kernel, first * rows), in_specs=[i...  11.7 us
    all_to_all x3, waiting for transfers between devices, exchange(): return lax.all_to_all(array, axes, 0, 0, tiled=True)  11.7 us
    pallas_call x1, Pallas kernels, layer(): pl.pallas_call(functools.partial(layer_kernel, back, chunk_rows), grid=(r...  5.3 us
    unnamed x16, local copies, waits for them, and re-layouts  3.64 us
  transfers between devices with their start and end apart: 10, of which 6 were waited for; matrix products, arithmetic and copies ran while one was open for 3% of the time, Pallas kernels for 13%

profile of v2, /device:TPU:1, one launch (start us, length us, event | category | flops | bytes accessed | tf_op | source)
XLA Modules:
  0.0 117.4 jit_solution(17527158169395734066)
XLA Ops:
  0.6 8.4 %collective-permute-start = (bf16[1024,128]{1,0:T(8,128)(2,1)}, bf16[1024,128]{1,0:T(8,128)(2,1)S(1)}, u32[]{:S(2)}, u32[]{:S(2)}) collective-permute-start(bf16[1024,128]{1,0:T(8,128)(2,1)} %own_ref.1), channel_id=1, source_target_pairs={{0,8},{1,9},{2,10},{3,11},{4,12},{5,13},{6,14},{7,15},{8,16},{9,17... | collective-permute-start | bytes 786440 | tf_op jit(solution)/shard_map/ppermute | solution.py:272
  9.1 5.8 %collective-permute-start.2 = (bf16[1024,128]{1,0:T(8,128)(2,1)}, bf16[1024,128]{1,0:T(8,128)(2,1)S(1)}, u32[]{:S(2)}, u32[]{:S(2)}) collective-permute-start(bf16[1024,128]{1,0:T(8,128)(2,1)} %own_ref.1), channel_id=1, source_target_pairs={{0,32},{1,33},{2,34},{3,35},{4,36},{5,37},{6,38},{7,39},{8,40},{9,... | collective-permute-start | bytes 786440 | tf_op jit(solution)/shard_map/ppermute | solution.py:272
  14.9 4.0 %collective-permute-start.1 = (bf16[1024,128]{1,0:T(8,128)(2,1)}, bf16[1024,128]{1,0:T(8,128)(2,1)S(1)}, u32[]{:S(2)}, u32[]{:S(2)}) collective-permute-start(bf16[1024,128]{1,0:T(8,128)(2,1)} %own_ref.1), channel_id=1, source_target_pairs={{0,16},{1,17},{2,18},{3,19},{4,20},{5,21},{6,22},{7,23},{8,24},{9,... | collective-permute-start | bytes 786440 | tf_op jit(solution)/shard_map/ppermute | solution.py:272
  18.9 0.8 copy-done.4
  19.7 7.0 %count_tiles.2.close_ref = bf16[3072,1024]{1,0:T(8,128)(2,1)S(1)} custom-call(s32[10,1024]{1,0:T(8,128)S(1)} %bitcast.4), custom_call_target="tpu_custom_call" | custom-call | flops 94371840 | bytes 6291456 | tf_op jit(solution)/shard_map/count_tiles/pallas_call | solution.py:64
  26.8 8.3 %collective-permute-done.refs_3_ = bf16[1024,128]{1,0:T(8,128)(2,1)S(1)} collective-permute-done((bf16[1024,128]{1,0:T(8,128)(2,1)}, bf16[1024,128]{1,0:T(8,128)(2,1)S(1)}, u32[]{:S(2)}, u32[]{:S(2)}) %collective-permute-start) | collective-permute-done | bytes 262176 | tf_op jit(solution)/shard_map/ppermute | solution.py:272
  35.1 1.9 %collective-permute-start.3 = (bf16[1024,128]{1,0:T(8,128)(2,1)S(1)}, bf16[1024,128]{1,0:T(8,128)(2,1)S(1)}, u32[]{:S(2)}, u32[]{:S(2)}) collective-permute-start(bf16[1024,128]{1,0:T(8,128)(2,1)S(1)} %collective-permute-done.refs_3_), channel_id=1, source_target_pairs={{0,16},{1,17},{2,18},{3,19},{4,20},{5,21},{6,22},{7,23},{8,24},{9,... | collective-permute-start | bytes 786440 | tf_op jit(solution)/shard_map/ppermute | solution.py:272
  37.0 4.7 %count_tiles.3.far_ref = bf16[2048,1024]{1,0:T(8,128)(2,1)S(1)} custom-call(s32[10,1024]{1,0:T(8,128)S(1)} %bitcast.5), custom_call_target="tpu_custom_call" | custom-call | flops 62914560 | bytes 4194304 | tf_op jit(solution)/shard_map/count_tiles/pallas_call | solution.py:64
  41.7 0.0 copy-start.3
  41.7 0.0 copy-start.7
  41.7 2.0 %collective-permute-done.1.refs_1_ = bf16[1024,128]{1,0:T(8,128)(2,1)S(1)} collective-permute-done((bf16[1024,128]{1,0:T(8,128)(2,1)}, bf16[1024,128]{1,0:T(8,128)(2,1)S(1)}, u32[]{:S(2)}, u32[]{:S(2)}) %collective-permute-start.1) | collective-permute-done | bytes 262176 | tf_op jit(solution)/shard_map/ppermute | solution.py:272
  43.8 1.3 %gather_sum.1.part_ref = f32[128,1024]{1,0:T(8,128)S(1)} custom-call(bf16[3072,1024]{1,0:T(8,128)(2,1)S(1)} %count_tiles.2.close_ref, bf16[2048,1024]{1,0:T(8,128)(2,1)S(1)} %count_tiles.3.far_ref, bf16[1024,128]{1,0:T(8,128)(2,1)S(1)} %copy-done.2, bf16[1024,128]{1,0:T(8,128)(2,1)S(1)} %collective-permute-done.1.refs_1_, ...), custom_call_target="tpu_custom_call" | custom-call | flops 1073741824 | bytes 1048576 | tf_op jit(solution)/shard_map/gather_sum/pallas_call | solution.py:99
  45.1 3.1 %collective-permute-done.3.block_ref = bf16[1024,128]{1,0:T(8,128)(2,1)S(1)} collective-permute-done((bf16[1024,128]{1,0:T(8,128)(2,1)S(1)}, bf16[1024,128]{1,0:T(8,128)(2,1)S(1)}, u32[]{:S(2)}, u32[]{:S(2)}) %collective-permute-start.3) | collective-permute-done | bytes 262176 | tf_op jit(solution)/shard_map/ppermute | solution.py:272
  48.1 5.3 %layer.1 = (bf16[1024,512]{1,0:T(8,128)(2,1)}, bf16[64,24,128]{2,1,0:T(8,128)(2,1)}, f32[1024,128]{1,0:T(8,128)S(1)}, bf16[1024,128]{1,0:T(8,128)(2,1)S(1)}, bf16[2048,128]{1,0:T(8,128)(2,1)S(1)}) custom-call(bf16[3072,1024]{1,0:T(8,128)(2,1)S(1)} %count_tiles.2.close_ref, bf16[2048,1024]{1,0:T(8,128)(2,1)S(1)} %count_tiles.3.far_ref, ...), custom_call_target="tpu_custom_call" | custom-call | flops 1610612736 | bytes 2097152 | tf_op jit(solution)/shard_map/layer/pallas_call | solution.py:194
  53.5 10.1 %all-to-all-start = ((bf16[64,24,128]{2,1,0:T(8,128)(2,1)}), bf16[64,24,128]{2,1,0:T(8,128)(2,1)S(1)}, u32[]{:S(2)}, u32[]{:S(2)}) async-start(bf16[64,24,128]{2,1,0:T(8,128)(2,1)} %get-tuple-element.27), calls=%async_computation | async-start | bytes 786432 | tf_op jit(solution)/shard_map/all_to_all | solution.py:276
  63.6 7.8 %collective-permute-start.4 = (bf16[2048,128]{1,0:T(8,128)(2,1)S(1)}, bf16[2048,128]{1,0:T(8,128)(2,1)S(1)}, u32[]{:S(2)}, u32[]{:S(2)}) collective-permute-start(bf16[2048,128]{1,0:T(8,128)(2,1)S(1)} %get-tuple-element.26), channel_id=1, source_target_pairs={{0,752},{1,753},{2,754},{3,755},{4,756},{5,757},{6,758},{7,759},{8... | collective-permute-start | bytes 1572872 | tf_op jit(solution)/shard_map/ppermute | solution.py:272
  71.4 2.8 %copy-done.1 = bf16[3072,1024]{1,0:T(8,128)(2,1)S(1)} copy-done((bf16[3072,1024]{1,0:T(8,128)(2,1)S(1)}, bf16[3072,1024]{1,0:T(8,128)(2,1)}, u32[]{:S(2)}) %copy-start.1) | copy-done | bytes 6291480
  74.2 1.8 %spread.1 = (f32[1024,128]{1,0:T(8,128)S(1)}, bf16[2048,128]{1,0:T(8,128)(2,1)S(1)}) custom-call(bf16[3072,1024]{1,0:T(8,128)(2,1)S(1)} %copy-done.1, bf16[1024,128]{1,0:T(8,128)(2,1)S(1)} %get-tuple-element.22.dmean_ref, f32[1024,128]{1,0:T(8,128)S(1)} %get-tuple-element.23.dself_ref), custom_call_target="tpu_custom_call" | custom-call | flops 805306368 | bytes 786432 | tf_op jit(solution)/shard_map/spread/pallas_call | solution.py:225
  76.0 2.2 %all-to-all-done = bf16[64,24,128]{2,1,0:T(8,128)(2,1)S(1)} async-done(((bf16[64,24,128]{2,1,0:T(8,128)(2,1)}), bf16[64,24,128]{2,1,0:T(8,128)(2,1)S(1)}, u32[]{:S(2)}, u32[]{:S(2)}) %all-to-all-start) | async-done | bytes 393248 | tf_op jit(solution)/shard_map/all_to_all | solution.py:276
  78.2 0.1 reduce_sum.21
  78.3 0.6 broadcast_in_dim.7
  78.9 5.7 %all-to-all-start.1 = ((bf16[12,24,128]{2,1,0:T(8,128)(2,1)}), bf16[12,24,128]{2,1,0:T(8,128)(2,1)S(1)}, u32[]{:S(2)}, u32[]{:S(2)}) async-start(bf16[12,24,128]{2,1,0:T(8,128)(2,1)} %broadcast_in_dim.7), calls=%async_computation.1 | async-start | bytes 147456 | tf_op jit(solution)/shard_map/all_to_all | solution.py:276
  84.6 0.1 add_convert_fusion
  84.8 10.8 %collective-permute-start.5 = (bf16[1024,128]{1,0:T(8,128)(2,1)S(1)}, bf16[1024,128]{1,0:T(8,128)(2,1)S(1)}, u32[]{:S(2)}, u32[]{:S(2)}) collective-permute-start(bf16[1024,128]{1,0:T(8,128)(2,1)S(1)} %get-tuple-element.31), channel_id=1, source_target_pairs={{0,760},{1,761},{2,762},{3,763},{4,764},{5,765},{6,766},{7,767},{8... | collective-permute-start | bytes 786440 | tf_op jit(solution)/shard_map/ppermute | solution.py:272
  95.6 1.9 %collective-permute-start.6 = (bf16[1024,128]{1,0:T(8,128)(2,1)S(1)}, bf16[1024,128]{1,0:T(8,128)(2,1)S(1)}, u32[]{:S(2)}, u32[]{:S(2)}) collective-permute-start(bf16[1024,128]{1,0:T(8,128)(2,1)S(1)} %get-tuple-element.32), channel_id=1, source_target_pairs={{0,752},{1,753},{2,754},{3,755},{4,756},{5,757},{6,758},{7,759},{8... | collective-permute-start | bytes 786440 | tf_op jit(solution)/shard_map/ppermute | solution.py:272
  97.6 0.7 broadcast_in_dim.8
  98.3 6.2 %all-to-all-start.2 = ((bf16[64,16,128]{2,1,0:T(8,128)(2,1)}), bf16[64,16,128]{2,1,0:T(8,128)(2,1)S(1)}, u32[]{:S(2)}, u32[]{:S(2)}) async-start(bf16[64,16,128]{2,1,0:T(8,128)(2,1)} %broadcast_in_dim.8), calls=%async_computation.2 | async-start | bytes 524288 | tf_op jit(solution)/shard_map/all_to_all | solution.py:276
  104.5 0.6 slice_bitcast_fusion
  105.1 1.2 %collective-permute-done.6 = bf16[1024,128]{1,0:T(8,128)(2,1)S(1)} collective-permute-done((bf16[1024,128]{1,0:T(8,128)(2,1)S(1)}, bf16[1024,128]{1,0:T(8,128)(2,1)S(1)}, u32[]{:S(2)}, u32[]{:S(2)}) %collective-permute-start.6) | collective-permute-done | bytes 262176 | tf_op jit(solution)/shard_map/ppermute | solution.py:272
  106.3 0.8 add_convert_fusion.1
  107.1 9.5 %all-to-all-done.2.chunks_ref = bf16[64,16,128]{2,1,0:T(8,128)(2,1)S(1)} async-done(((bf16[64,16,128]{2,1,0:T(8,128)(2,1)}), bf16[64,16,128]{2,1,0:T(8,128)(2,1)S(1)}, u32[]{:S(2)}, u32[]{:S(2)}) %all-to-all-start.2) | async-done | bytes 262176 | tf_op jit(solution)/shard_map/all_to_all | solution.py:276
  116.6 0.8 unfold.1
  (20 shorter events, 0.1 us)
Async XLA Ops:
  0.6 43.1 %copy-start.2 = (bf16[1024,128]{1,0:T(8,128)(2,1)S(1)}, bf16[1024,128]{1,0:T(8,128)(2,1)}, u32[]{:S(2)}) copy-start(bf16[1024,128]{1,0:T(8,128)(2,1)} %own_ref.1) | copy-start | bytes 786436
  0.6 34.4 %collective-permute-start = (bf16[1024,128]{1,0:T(8,128)(2,1)}, bf16[1024,128]{1,0:T(8,128)(2,1)S(1)}, u32[]{:S(2)}, u32[]{:S(2)}) collective-permute-start(bf16[1024,128]{1,0:T(8,128)(2,1)} %own_ref.1), channel_id=1, source_target_pairs={{0,8},{1,9},{2,10},{3,11},{4,12},{5,13},{6,14},{7,15},{8,16},{9,17... | collective-permute-start | bytes 786440 | tf_op jit(solution)/shard_map/ppermute | solution.py:272
  9.1 32.7 %collective-permute-start.2 = (bf16[1024,128]{1,0:T(8,128)(2,1)}, bf16[1024,128]{1,0:T(8,128)(2,1)S(1)}, u32[]{:S(2)}, u32[]{:S(2)}) collective-permute-start(bf16[1024,128]{1,0:T(8,128)(2,1)} %own_ref.1), channel_id=1, source_target_pairs={{0,32},{1,33},{2,34},{3,35},{4,36},{5,37},{6,38},{7,39},{8,40},{9,... | collective-permute-start | bytes 786440 | tf_op jit(solution)/shard_map/ppermute | solution.py:272
  14.9 28.9 %collective-permute-start.1 = (bf16[1024,128]{1,0:T(8,128)(2,1)}, bf16[1024,128]{1,0:T(8,128)(2,1)S(1)}, u32[]{:S(2)}, u32[]{:S(2)}) collective-permute-start(bf16[1024,128]{1,0:T(8,128)(2,1)} %own_ref.1), channel_id=1, source_target_pairs={{0,16},{1,17},{2,18},{3,19},{4,20},{5,21},{6,22},{7,23},{8,24},{9,... | collective-permute-start | bytes 786440 | tf_op jit(solution)/shard_map/ppermute | solution.py:272
  18.9 0.8 copy-start.4
  26.7 21.4 %copy-start = (bf16[3072,1024]{1,0:T(8,128)(2,1)}, bf16[3072,1024]{1,0:T(8,128)(2,1)S(1)}, u32[]{:S(2)}) copy-start(bf16[3072,1024]{1,0:T(8,128)(2,1)S(1)} %count_tiles.2.close_ref) | copy-start | bytes 18874372
  35.1 13.0 %collective-permute-start.3 = (bf16[1024,128]{1,0:T(8,128)(2,1)S(1)}, bf16[1024,128]{1,0:T(8,128)(2,1)S(1)}, u32[]{:S(2)}, u32[]{:S(2)}) collective-permute-start(bf16[1024,128]{1,0:T(8,128)(2,1)S(1)} %collective-permute-done.refs_3_), channel_id=1, source_target_pairs={{0,16},{1,17},{2,18},{3,19},{4,20},{5,21},{6,22},{7,23},{8,24},{9,... | collective-permute-start | bytes 786440 | tf_op jit(solution)/shard_map/ppermute | solution.py:272
  41.7 6.4 %copy-start.3 = (bf16[1024,512]{1,0:T(8,128)(2,1)S(1)}, bf16[1024,512]{1,0:T(8,128)(2,1)}, u32[]{:S(2)}) copy-start(bf16[1024,512]{1,0:T(8,128)(2,1)} %cot_ref.1) | copy-start | bytes 3145732
  41.7 6.4 %copy-start.5 = (bf16[128,512]{1,0:T(8,128)(2,1)S(1)}, bf16[128,512]{1,0:T(8,128)(2,1)}, u32[]{:S(2)}) copy-start(bf16[128,512]{1,0:T(8,128)(2,1)} %w_self_ref.1) | copy-start | bytes 393220
  41.7 6.4 %copy-start.6 = (bf16[128,512]{1,0:T(8,128)(2,1)S(1)}, bf16[128,512]{1,0:T(8,128)(2,1)}, u32[]{:S(2)}) copy-start(bf16[128,512]{1,0:T(8,128)(2,1)} %w_neigh_ref.1) | copy-start | bytes 393220
  41.7 6.4 %copy-start.7 = (f32[512]{0:T(512)S(1)}, f32[512]{0:T(512)}, u32[]{:S(2)}) copy-start(f32[512]{0:T(512)} %param.10) | copy-start | bytes 6148
  53.5 24.7 %all-to-all-start = ((bf16[64,24,128]{2,1,0:T(8,128)(2,1)}), bf16[64,24,128]{2,1,0:T(8,128)(2,1)S(1)}, u32[]{:S(2)}, u32[]{:S(2)}) async-start(bf16[64,24,128]{2,1,0:T(8,128)(2,1)} %get-tuple-element.27), calls=%async_computation | async-start | bytes 786432 | tf_op jit(solution)/shard_map/all_to_all | solution.py:276
  63.6 21.0 %collective-permute-start.4 = (bf16[2048,128]{1,0:T(8,128)(2,1)S(1)}, bf16[2048,128]{1,0:T(8,128)(2,1)S(1)}, u32[]{:S(2)}, u32[]{:S(2)}) collective-permute-start(bf16[2048,128]{1,0:T(8,128)(2,1)S(1)} %get-tuple-element.26), channel_id=1, source_target_pairs={{0,752},{1,753},{2,754},{3,755},{4,756},{5,757},{6,758},{7,759},{8... | collective-permute-start | bytes 1572872 | tf_op jit(solution)/shard_map/ppermute | solution.py:272
  71.4 2.8 %copy-start.1 = (bf16[3072,1024]{1,0:T(8,128)(2,1)S(1)}, bf16[3072,1024]{1,0:T(8,128)(2,1)}, u32[]{:S(2)}) copy-start(bf16[3072,1024]{1,0:T(8,128)(2,1)} %copy-done) | copy-start | bytes 18874372
  78.9 18.6 %all-to-all-start.1 = ((bf16[12,24,128]{2,1,0:T(8,128)(2,1)}), bf16[12,24,128]{2,1,0:T(8,128)(2,1)S(1)}, u32[]{:S(2)}, u32[]{:S(2)}) async-start(bf16[12,24,128]{2,1,0:T(8,128)(2,1)} %broadcast_in_dim.7), calls=%async_computation.1 | async-start | bytes 147456 | tf_op jit(solution)/shard_map/all_to_all | solution.py:276
  84.8 20.3 %collective-permute-start.5 = (bf16[1024,128]{1,0:T(8,128)(2,1)S(1)}, bf16[1024,128]{1,0:T(8,128)(2,1)S(1)}, u32[]{:S(2)}, u32[]{:S(2)}) collective-permute-start(bf16[1024,128]{1,0:T(8,128)(2,1)S(1)} %get-tuple-element.31), channel_id=1, source_target_pairs={{0,760},{1,761},{2,762},{3,763},{4,764},{5,765},{6,766},{7,767},{8... | collective-permute-start | bytes 786440 | tf_op jit(solution)/shard_map/ppermute | solution.py:272
  95.6 10.7 %collective-permute-start.6 = (bf16[1024,128]{1,0:T(8,128)(2,1)S(1)}, bf16[1024,128]{1,0:T(8,128)(2,1)S(1)}, u32[]{:S(2)}, u32[]{:S(2)}) collective-permute-start(bf16[1024,128]{1,0:T(8,128)(2,1)S(1)} %get-tuple-element.32), channel_id=1, source_target_pairs={{0,752},{1,753},{2,754},{3,755},{4,756},{5,757},{6,758},{7,759},{8... | collective-permute-start | bytes 786440 | tf_op jit(solution)/shard_map/ppermute | solution.py:272
  98.3 18.2 %all-to-all-start.2 = ((bf16[64,16,128]{2,1,0:T(8,128)(2,1)}), bf16[64,16,128]{2,1,0:T(8,128)(2,1)S(1)}, u32[]{:S(2)}, u32[]{:S(2)}) async-start(bf16[64,16,128]{2,1,0:T(8,128)(2,1)} %broadcast_in_dim.8), calls=%async_computation.2 | async-start | bytes 524288 | tf_op jit(solution)/shard_map/all_to_all | solution.py:276

commit v3 on v2

--- a/solution.py
+++ b/solution.py
@@ -290,9 +290,10 @@
     n_first = lax.axis_size(FIRST)
     near1 = shifted(features, 1)
     near2 = shifted(features, 2)
-    near4 = shifted(features, 4)
     entries = neighbours.T
     tiles = count_tiles(entries, 0, CLOSE)
+    near2, tiles = lax.optimization_barrier((near2, tiles))
+    near4 = shifted(near2, 2)
     near1, tiles, entries = lax.optimization_barrier((near1, tiles, entries))
     tiles = (tiles, count_tiles(entries, CLOSE, STEPS + 1 - CLOSE))
     near3 = shifted(near1, 2)

time: 118 us -> 114 us (0.966)
  starting transfers between devices: 62.6 us -> 50.8 us
  waiting for transfers between devices: 26.3 us -> 34.5 us
    ppermute x7, starting transfers between devices: 40.6 us -> 33.3 us  [shifted(): return lax.ppermute(array, AXES, shift_pairs(by))]
    ppermute x7, waiting for transfers between devices: 14.6 us -> 20.7 us  [shifted(): return lax.ppermute(array, AXES, shift_pairs(by))]
    all_to_all x3, starting transfers between devices: 22 us -> 17.5 us  [exchange(): return lax.all_to_all(array, axes, 0, 0, tiled=True)]
    all_to_all x3, waiting for transfers between devices: 11.7 us -> 13.9 us  [exchange(): return lax.all_to_all(array, axes, 0, 0, tiled=True)]
where the time goes in v3:
time: 114 us
  starting transfers between devices  50.8 us (45%)
  waiting for transfers between devices  34.5 us (30%)
  Pallas kernels  20.9 us (18%)
  local copies, waits for them, and re-layouts  5.65 us (5%)
    ppermute x7, starting transfers between devices, shifted(): return lax.ppermute(array, AXES, shift_pairs(by))  33.3 us
    ppermute x7, waiting for transfers between devices, shifted(): return lax.ppermute(array, AXES, shift_pairs(by))  20.7 us
    all_to_all x3, starting transfers between devices, exchange(): return lax.all_to_all(array, axes, 0, 0, tiled=True)  17.5 us
    all_to_all x3, waiting for transfers between devices, exchange(): return lax.all_to_all(array, axes, 0, 0, tiled=True)  13.9 us
    pallas_call x2, Pallas kernels, count_tiles(): pl.pallas_call(functools.partial(count_kernel, first * rows), in_specs=[i...  11.7 us
    pallas_call x1, Pallas kernels, layer(): pl.pallas_call(functools.partial(layer_kernel, back, chunk_rows), grid=(r...  5.3 us
    unnamed x16, local copies, waits for them, and re-layouts  3.64 us
  transfers between devices with their start and end apart: 10, of which 6 were waited for; matrix products, arithmetic and copies ran while one was open for 3% of the time, Pallas kernels for 13%

profile of v3, /device:TPU:1, one launch (start us, length us, event | category | flops | bytes accessed | tf_op | source)
XLA Modules:
  0.0 113.8 jit_solution(6499551010896926097)
XLA Ops:
  0.6 5.0 %collective-permute-start.1 = (bf16[1024,128]{1,0:T(8,128)(2,1)}, bf16[1024,128]{1,0:T(8,128)(2,1)S(1)}, u32[]{:S(2)}, u32[]{:S(2)}) collective-permute-start(bf16[1024,128]{1,0:T(8,128)(2,1)} %own_ref.1), channel_id=1, source_target_pairs={{0,16},{1,17},{2,18},{3,19},{4,20},{5,21},{6,22},{7,23},{8,24},{9,... | collective-permute-start | bytes 786440 | tf_op jit(solution)/shard_map/ppermute | solution.py:272
  5.6 7.5 %collective-permute-start = (bf16[1024,128]{1,0:T(8,128)(2,1)}, bf16[1024,128]{1,0:T(8,128)(2,1)S(1)}, u32[]{:S(2)}, u32[]{:S(2)}) collective-permute-start(bf16[1024,128]{1,0:T(8,128)(2,1)} %own_ref.1), channel_id=1, source_target_pairs={{0,8},{1,9},{2,10},{3,11},{4,12},{5,13},{6,14},{7,15},{8,16},{9,17... | collective-permute-start | bytes 786440 | tf_op jit(solution)/shard_map/ppermute | solution.py:272
  13.1 0.8 copy-done.4
  13.9 7.0 %count_tiles.2.close_ref = bf16[3072,1024]{1,0:T(8,128)(2,1)S(1)} custom-call(s32[10,1024]{1,0:T(8,128)S(1)} %bitcast.4), custom_call_target="tpu_custom_call" | custom-call | flops 94371840 | bytes 6291456 | tf_op jit(solution)/shard_map/count_tiles/pallas_call | solution.py:64
  20.9 3.4 %collective-permute-done.1.refs_1_ = bf16[1024,128]{1,0:T(8,128)(2,1)S(1)} collective-permute-done((bf16[1024,128]{1,0:T(8,128)(2,1)}, bf16[1024,128]{1,0:T(8,128)(2,1)S(1)}, u32[]{:S(2)}, u32[]{:S(2)}) %collective-permute-start.1) | collective-permute-done | bytes 262176 | tf_op jit(solution)/shard_map/ppermute | solution.py:272
  24.3 1.9 %collective-permute-start.2 = (bf16[1024,128]{1,0:T(8,128)(2,1)S(1)}, bf16[1024,128]{1,0:T(8,128)(2,1)S(1)}, u32[]{:S(2)}, u32[]{:S(2)}) collective-permute-start(bf16[1024,128]{1,0:T(8,128)(2,1)S(1)} %collective-permute-done.1.refs_1_), channel_id=1, source_target_pairs={{0,16},{1,17},{2,18},{3,19},{4,20},{5,21},{6,22},{7,23},{8,24},{9,... | collective-permute-start | bytes 786440 | tf_op jit(solution)/shard_map/ppermute | solution.py:272
  26.3 13.1 %collective-permute-done.refs_3_ = bf16[1024,128]{1,0:T(8,128)(2,1)S(1)} collective-permute-done((bf16[1024,128]{1,0:T(8,128)(2,1)}, bf16[1024,128]{1,0:T(8,128)(2,1)S(1)}, u32[]{:S(2)}, u32[]{:S(2)}) %collective-permute-start) | collective-permute-done | bytes 262176 | tf_op jit(solution)/shard_map/ppermute | solution.py:272
  39.4 1.9 %collective-permute-start.3 = (bf16[1024,128]{1,0:T(8,128)(2,1)S(1)}, bf16[1024,128]{1,0:T(8,128)(2,1)S(1)}, u32[]{:S(2)}, u32[]{:S(2)}) collective-permute-start(bf16[1024,128]{1,0:T(8,128)(2,1)S(1)} %collective-permute-done.refs_3_), channel_id=1, source_target_pairs={{0,16},{1,17},{2,18},{3,19},{4,20},{5,21},{6,22},{7,23},{8,24},{9,... | collective-permute-start | bytes 786440 | tf_op jit(solution)/shard_map/ppermute | solution.py:272
  41.3 4.7 %count_tiles.3.far_ref = bf16[2048,1024]{1,0:T(8,128)(2,1)S(1)} custom-call(s32[10,1024]{1,0:T(8,128)S(1)} %bitcast.5), custom_call_target="tpu_custom_call" | custom-call | flops 62914560 | bytes 4194304 | tf_op jit(solution)/shard_map/count_tiles/pallas_call | solution.py:64
  46.0 0.0 copy-start.6
  46.0 0.0 copy-start.7
  46.0 1.3 %gather_sum.1.part_ref = f32[128,1024]{1,0:T(8,128)S(1)} custom-call(bf16[3072,1024]{1,0:T(8,128)(2,1)S(1)} %count_tiles.2.close_ref, bf16[2048,1024]{1,0:T(8,128)(2,1)S(1)} %count_tiles.3.far_ref, bf16[1024,128]{1,0:T(8,128)(2,1)S(1)} %copy-done.2, bf16[1024,128]{1,0:T(8,128)(2,1)S(1)} %collective-permute-done.1.refs_1_, ...), custom_call_target="tpu_custom_call" | custom-call | flops 1073741824 | bytes 1048576 | tf_op jit(solution)/shard_map/gather_sum/pallas_call | solution.py:99
  47.4 2.4 %collective-permute-done.3.block_ref = bf16[1024,128]{1,0:T(8,128)(2,1)S(1)} collective-permute-done((bf16[1024,128]{1,0:T(8,128)(2,1)S(1)}, bf16[1024,128]{1,0:T(8,128)(2,1)S(1)}, u32[]{:S(2)}, u32[]{:S(2)}) %collective-permute-start.3) | collective-permute-done | bytes 262176 | tf_op jit(solution)/shard_map/ppermute | solution.py:272
  49.8 5.3 %layer.1 = (bf16[1024,512]{1,0:T(8,128)(2,1)}, bf16[64,24,128]{2,1,0:T(8,128)(2,1)}, f32[1024,128]{1,0:T(8,128)S(1)}, bf16[1024,128]{1,0:T(8,128)(2,1)S(1)}, bf16[2048,128]{1,0:T(8,128)(2,1)S(1)}) custom-call(bf16[3072,1024]{1,0:T(8,128)(2,1)S(1)} %count_tiles.2.close_ref, bf16[2048,1024]{1,0:T(8,128)(2,1)S(1)} %count_tiles.3.far_ref, ...), custom_call_target="tpu_custom_call" | custom-call | flops 1610612736 | bytes 2097152 | tf_op jit(solution)/shard_map/layer/pallas_call | solution.py:194
  55.1 7.9 %all-to-all-start = ((bf16[64,24,128]{2,1,0:T(8,128)(2,1)}), bf16[64,24,128]{2,1,0:T(8,128)(2,1)S(1)}, u32[]{:S(2)}, u32[]{:S(2)}) async-start(bf16[64,24,128]{2,1,0:T(8,128)(2,1)} %get-tuple-element.31), calls=%async_computation | async-start | bytes 786432 | tf_op jit(solution)/shard_map/all_to_all | solution.py:276
  63.1 5.2 %collective-permute-start.4 = (bf16[2048,128]{1,0:T(8,128)(2,1)S(1)}, bf16[2048,128]{1,0:T(8,128)(2,1)S(1)}, u32[]{:S(2)}, u32[]{:S(2)}) collective-permute-start(bf16[2048,128]{1,0:T(8,128)(2,1)S(1)} %get-tuple-element.30), channel_id=1, source_target_pairs={{0,752},{1,753},{2,754},{3,755},{4,756},{5,757},{6,758},{7,759},{8... | collective-permute-start | bytes 1572872 | tf_op jit(solution)/shard_map/ppermute | solution.py:272
  68.3 2.8 %copy-done.1 = bf16[3072,1024]{1,0:T(8,128)(2,1)S(1)} copy-done((bf16[3072,1024]{1,0:T(8,128)(2,1)S(1)}, bf16[3072,1024]{1,0:T(8,128)(2,1)}, u32[]{:S(2)}) %copy-start.1) | copy-done | bytes 6291480
  71.0 1.8 %spread.1 = (f32[1024,128]{1,0:T(8,128)S(1)}, bf16[2048,128]{1,0:T(8,128)(2,1)S(1)}) custom-call(bf16[3072,1024]{1,0:T(8,128)(2,1)S(1)} %copy-done.1, bf16[1024,128]{1,0:T(8,128)(2,1)S(1)} %get-tuple-element.26.dmean_ref, f32[1024,128]{1,0:T(8,128)S(1)} %get-tuple-element.27.dself_ref), custom_call_target="tpu_custom_call" | custom-call | flops 805306368 | bytes 786432 | tf_op jit(solution)/shard_map/spread/pallas_call | solution.py:225
  72.8 5.0 %all-to-all-done = bf16[64,24,128]{2,1,0:T(8,128)(2,1)S(1)} async-done(((bf16[64,24,128]{2,1,0:T(8,128)(2,1)}), bf16[64,24,128]{2,1,0:T(8,128)(2,1)S(1)}, u32[]{:S(2)}, u32[]{:S(2)}) %all-to-all-start) | async-done | bytes 393248 | tf_op jit(solution)/shard_map/all_to_all | solution.py:276
  77.8 0.1 reduce_sum.21
  77.9 0.6 broadcast_in_dim.7
  78.5 3.8 %all-to-all-start.1 = ((bf16[12,24,128]{2,1,0:T(8,128)(2,1)}), bf16[12,24,128]{2,1,0:T(8,128)(2,1)S(1)}, u32[]{:S(2)}, u32[]{:S(2)}) async-start(bf16[12,24,128]{2,1,0:T(8,128)(2,1)} %broadcast_in_dim.7), calls=%async_computation.1 | async-start | bytes 147456 | tf_op jit(solution)/shard_map/all_to_all | solution.py:276
  82.3 0.1 add_convert_fusion
  82.5 9.9 %collective-permute-start.5 = (bf16[1024,128]{1,0:T(8,128)(2,1)S(1)}, bf16[1024,128]{1,0:T(8,128)(2,1)S(1)}, u32[]{:S(2)}, u32[]{:S(2)}) collective-permute-start(bf16[1024,128]{1,0:T(8,128)(2,1)S(1)} %get-tuple-element.35), channel_id=1, source_target_pairs={{0,760},{1,761},{2,762},{3,763},{4,764},{5,765},{6,766},{7,767},{8... | collective-permute-start | bytes 786440 | tf_op jit(solution)/shard_map/ppermute | solution.py:272
  92.5 1.9 %collective-permute-start.6 = (bf16[1024,128]{1,0:T(8,128)(2,1)S(1)}, bf16[1024,128]{1,0:T(8,128)(2,1)S(1)}, u32[]{:S(2)}, u32[]{:S(2)}) collective-permute-start(bf16[1024,128]{1,0:T(8,128)(2,1)S(1)} %get-tuple-element.36), channel_id=1, source_target_pairs={{0,752},{1,753},{2,754},{3,755},{4,756},{5,757},{6,758},{7,759},{8... | collective-permute-start | bytes 786440 | tf_op jit(solution)/shard_map/ppermute | solution.py:272
  94.4 0.7 broadcast_in_dim.8
  95.2 5.8 %all-to-all-start.2 = ((bf16[64,16,128]{2,1,0:T(8,128)(2,1)}), bf16[64,16,128]{2,1,0:T(8,128)(2,1)S(1)}, u32[]{:S(2)}, u32[]{:S(2)}) async-start(bf16[64,16,128]{2,1,0:T(8,128)(2,1)} %broadcast_in_dim.8), calls=%async_computation.2 | async-start | bytes 524288 | tf_op jit(solution)/shard_map/all_to_all | solution.py:276
  101.0 0.6 slice_bitcast_fusion
  101.6 1.7 %collective-permute-done.6 = bf16[1024,128]{1,0:T(8,128)(2,1)S(1)} collective-permute-done((bf16[1024,128]{1,0:T(8,128)(2,1)S(1)}, bf16[1024,128]{1,0:T(8,128)(2,1)S(1)}, u32[]{:S(2)}, u32[]{:S(2)}) %collective-permute-start.6) | collective-permute-done | bytes 262176 | tf_op jit(solution)/shard_map/ppermute | solution.py:272
  103.3 0.8 add_convert_fusion.1
  104.1 8.9 %all-to-all-done.2.chunks_ref = bf16[64,16,128]{2,1,0:T(8,128)(2,1)S(1)} async-done(((bf16[64,16,128]{2,1,0:T(8,128)(2,1)}), bf16[64,16,128]{2,1,0:T(8,128)(2,1)S(1)}, u32[]{:S(2)}, u32[]{:S(2)}) %all-to-all-start.2) | async-done | bytes 262176 | tf_op jit(solution)/shard_map/all_to_all | solution.py:276
  113.0 0.8 unfold.1
  (20 shorter events, 0.1 us)
Async XLA Ops:
  0.6 45.4 %copy-start.2 = (bf16[1024,128]{1,0:T(8,128)(2,1)S(1)}, bf16[1024,128]{1,0:T(8,128)(2,1)}, u32[]{:S(2)}) copy-start(bf16[1024,128]{1,0:T(8,128)(2,1)} %own_ref.1) | copy-start | bytes 786436
  0.6 23.7 %collective-permute-start.1 = (bf16[1024,128]{1,0:T(8,128)(2,1)}, bf16[1024,128]{1,0:T(8,128)(2,1)S(1)}, u32[]{:S(2)}, u32[]{:S(2)}) collective-permute-start(bf16[1024,128]{1,0:T(8,128)(2,1)} %own_ref.1), channel_id=1, source_target_pairs={{0,16},{1,17},{2,18},{3,19},{4,20},{5,21},{6,22},{7,23},{8,24},{9,... | collective-permute-start | bytes 786440 | tf_op jit(solution)/shard_map/ppermute | solution.py:272
  5.6 33.8 %collective-permute-start = (bf16[1024,128]{1,0:T(8,128)(2,1)}, bf16[1024,128]{1,0:T(8,128)(2,1)S(1)}, u32[]{:S(2)}, u32[]{:S(2)}) collective-permute-start(bf16[1024,128]{1,0:T(8,128)(2,1)} %own_ref.1), channel_id=1, source_target_pairs={{0,8},{1,9},{2,10},{3,11},{4,12},{5,13},{6,14},{7,15},{8,16},{9,17... | collective-permute-start | bytes 786440 | tf_op jit(solution)/shard_map/ppermute | solution.py:272
  13.1 0.8 copy-start.4
  20.9 28.9 %copy-start = (bf16[3072,1024]{1,0:T(8,128)(2,1)}, bf16[3072,1024]{1,0:T(8,128)(2,1)S(1)}, u32[]{:S(2)}) copy-start(bf16[3072,1024]{1,0:T(8,128)(2,1)S(1)} %count_tiles.2.close_ref) | copy-start | bytes 18874372
  24.3 21.7 %collective-permute-start.2 = (bf16[1024,128]{1,0:T(8,128)(2,1)S(1)}, bf16[1024,128]{1,0:T(8,128)(2,1)S(1)}, u32[]{:S(2)}, u32[]{:S(2)}) collective-permute-start(bf16[1024,128]{1,0:T(8,128)(2,1)S(1)} %collective-permute-done.1.refs_1_), channel_id=1, source_target_pairs={{0,16},{1,17},{2,18},{3,19},{4,20},{5,21},{6,22},{7,23},{8,24},{9,... | collective-permute-start | bytes 786440 | tf_op jit(solution)/shard_map/ppermute | solution.py:272
  39.4 10.4 %collective-permute-start.3 = (bf16[1024,128]{1,0:T(8,128)(2,1)S(1)}, bf16[1024,128]{1,0:T(8,128)(2,1)S(1)}, u32[]{:S(2)}, u32[]{:S(2)}) collective-permute-start(bf16[1024,128]{1,0:T(8,128)(2,1)S(1)} %collective-permute-done.refs_3_), channel_id=1, source_target_pairs={{0,16},{1,17},{2,18},{3,19},{4,20},{5,21},{6,22},{7,23},{8,24},{9,... | collective-permute-start | bytes 786440 | tf_op jit(solution)/shard_map/ppermute | solution.py:272
  46.0 3.8 %copy-start.3 = (bf16[1024,512]{1,0:T(8,128)(2,1)S(1)}, bf16[1024,512]{1,0:T(8,128)(2,1)}, u32[]{:S(2)}) copy-start(bf16[1024,512]{1,0:T(8,128)(2,1)} %cot_ref.1) | copy-start | bytes 3145732
  46.0 3.8 %copy-start.5 = (bf16[128,512]{1,0:T(8,128)(2,1)S(1)}, bf16[128,512]{1,0:T(8,128)(2,1)}, u32[]{:S(2)}) copy-start(bf16[128,512]{1,0:T(8,128)(2,1)} %w_self_ref.1) | copy-start | bytes 393220
  46.0 3.8 %copy-start.6 = (bf16[128,512]{1,0:T(8,128)(2,1)S(1)}, bf16[128,512]{1,0:T(8,128)(2,1)}, u32[]{:S(2)}) copy-start(bf16[128,512]{1,0:T(8,128)(2,1)} %w_neigh_ref.1) | copy-start | bytes 393220
  46.0 3.8 %copy-start.7 = (f32[512]{0:T(512)S(1)}, f32[512]{0:T(512)}, u32[]{:S(2)}) copy-start(f32[512]{0:T(512)} %param.10) | copy-start | bytes 6148
  55.1 22.7 %all-to-all-start = ((bf16[64,24,128]{2,1,0:T(8,128)(2,1)}), bf16[64,24,128]{2,1,0:T(8,128)(2,1)S(1)}, u32[]{:S(2)}, u32[]{:S(2)}) async-start(bf16[64,24,128]{2,1,0:T(8,128)(2,1)} %get-tuple-element.31), calls=%async_computation | async-start | bytes 786432 | tf_op jit(solution)/shard_map/all_to_all | solution.py:276
  63.1 19.2 %collective-permute-start.4 = (bf16[2048,128]{1,0:T(8,128)(2,1)S(1)}, bf16[2048,128]{1,0:T(8,128)(2,1)S(1)}, u32[]{:S(2)}, u32[]{:S(2)}) collective-permute-start(bf16[2048,128]{1,0:T(8,128)(2,1)S(1)} %get-tuple-element.30), channel_id=1, source_target_pairs={{0,752},{1,753},{2,754},{3,755},{4,756},{5,757},{6,758},{7,759},{8... | collective-permute-start | bytes 1572872 | tf_op jit(solution)/shard_map/ppermute | solution.py:272
  68.2 2.8 %copy-start.1 = (bf16[3072,1024]{1,0:T(8,128)(2,1)S(1)}, bf16[3072,1024]{1,0:T(8,128)(2,1)}, u32[]{:S(2)}) copy-start(bf16[3072,1024]{1,0:T(8,128)(2,1)} %copy-done) | copy-start | bytes 18874372
  78.5 15.9 %all-to-all-start.1 = ((bf16[12,24,128]{2,1,0:T(8,128)(2,1)}), bf16[12,24,128]{2,1,0:T(8,128)(2,1)S(1)}, u32[]{:S(2)}, u32[]{:S(2)}) async-start(bf16[12,24,128]{2,1,0:T(8,128)(2,1)} %broadcast_in_dim.7), calls=%async_computation.1 | async-start | bytes 147456 | tf_op jit(solution)/shard_map/all_to_all | solution.py:276
  82.5 19.1 %collective-permute-start.5 = (bf16[1024,128]{1,0:T(8,128)(2,1)S(1)}, bf16[1024,128]{1,0:T(8,128)(2,1)S(1)}, u32[]{:S(2)}, u32[]{:S(2)}) collective-permute-start(bf16[1024,128]{1,0:T(8,128)(2,1)S(1)} %get-tuple-element.35), channel_id=1, source_target_pairs={{0,760},{1,761},{2,762},{3,763},{4,764},{5,765},{6,766},{7,767},{8... | collective-permute-start | bytes 786440 | tf_op jit(solution)/shard_map/ppermute | solution.py:272
  92.5 10.8 %collective-permute-start.6 = (bf16[1024,128]{1,0:T(8,128)(2,1)S(1)}, bf16[1024,128]{1,0:T(8,128)(2,1)S(1)}, u32[]{:S(2)}, u32[]{:S(2)}) collective-permute-start(bf16[1024,128]{1,0:T(8,128)(2,1)S(1)} %get-tuple-element.36), channel_id=1, source_target_pairs={{0,752},{1,753},{2,754},{3,755},{4,756},{5,757},{6,758},{7,759},{8... | collective-permute-start | bytes 786440 | tf_op jit(solution)/shard_map/ppermute | solution.py:272
  95.2 17.8 %all-to-all-start.2 = ((bf16[64,16,128]{2,1,0:T(8,128)(2,1)}), bf16[64,16,128]{2,1,0:T(8,128)(2,1)S(1)}, u32[]{:S(2)}, u32[]{:S(2)}) async-start(bf16[64,16,128]{2,1,0:T(8,128)(2,1)} %broadcast_in_dim.8), calls=%async_computation.2 | async-start | bytes 524288 | tf_op jit(solution)/shard_map/all_to_all | solution.py:276

commit v4 on v3

--- a/solution.py
+++ b/solution.py
@@ -13,7 +13,7 @@
 STEPS = 4
 CLOSE = 3
 WINDOW_TILE = 256
-NODE_TILE = 256
+NODE_TILE = 512
 LANES = 128
 SUBLANES = 8
 PACK = 16

time: 114 us -> 114 us (level)
  no operation moved by 1% of the time
where the time goes in v4:
time: 114 us; the launch traced here: 113 us
  starting transfers between devices  50.8 us (45%)
  waiting for transfers between devices  34.5 us (30%)
  Pallas kernels  20.2 us (18%)
  local copies, waits for them, and re-layouts  5.65 us (5%)
    ppermute x7, starting transfers between devices, shifted(): return lax.ppermute(array, AXES, shift_pairs(by))  33.3 us
    ppermute x7, waiting for transfers between devices, shifted(): return lax.ppermute(array, AXES, shift_pairs(by))  20.7 us
    all_to_all x3, starting transfers between devices, exchange(): return lax.all_to_all(array, axes, 0, 0, tiled=True)  17.5 us
    all_to_all x3, waiting for transfers between devices, exchange(): return lax.all_to_all(array, axes, 0, 0, tiled=True)  13.9 us
    pallas_call x2, Pallas kernels, count_tiles(): pl.pallas_call(functools.partial(count_kernel, first * rows), in_specs=[i...  11.7 us
    pallas_call x1, Pallas kernels, layer(): pl.pallas_call(functools.partial(layer_kernel, back, chunk_rows), grid=(r...  4.6 us
    unnamed x16, local copies, waits for them, and re-layouts  3.64 us
  transfers between devices with their start and end apart: 10, of which 6 were waited for; matrix products, arithmetic and copies ran while one was open for 3% of the time, Pallas kernels for 13%

profile of v4, /device:TPU:1, one launch (start us, length us, event | category | flops | bytes accessed | tf_op | source)
XLA Modules:
  0.0 113.1 jit_solution(2754759732112393211)
XLA Ops:
  0.6 5.0 %collective-permute-start.1 = (bf16[1024,128]{1,0:T(8,128)(2,1)}, bf16[1024,128]{1,0:T(8,128)(2,1)S(1)}, u32[]{:S(2)}, u32[]{:S(2)}) collective-permute-start(bf16[1024,128]{1,0:T(8,128)(2,1)} %own_ref.1), channel_id=1, source_target_pairs={{0,16},{1,17},{2,18},{3,19},{4,20},{5,21},{6,22},{7,23},{8,24},{9,... | collective-permute-start | bytes 786440 | tf_op jit(solution)/shard_map/ppermute | solution.py:272
  5.6 7.5 %collective-permute-start = (bf16[1024,128]{1,0:T(8,128)(2,1)}, bf16[1024,128]{1,0:T(8,128)(2,1)S(1)}, u32[]{:S(2)}, u32[]{:S(2)}) collective-permute-start(bf16[1024,128]{1,0:T(8,128)(2,1)} %own_ref.1), channel_id=1, source_target_pairs={{0,8},{1,9},{2,10},{3,11},{4,12},{5,13},{6,14},{7,15},{8,16},{9,17... | collective-permute-start | bytes 786440 | tf_op jit(solution)/shard_map/ppermute | solution.py:272
  13.1 0.8 copy-done.4
  13.9 7.0 %count_tiles.2.close_ref = bf16[3072,1024]{1,0:T(8,128)(2,1)S(1)} custom-call(s32[10,1024]{1,0:T(8,128)S(1)} %bitcast.4), custom_call_target="tpu_custom_call" | custom-call | flops 94371840 | bytes 6291456 | tf_op jit(solution)/shard_map/count_tiles/pallas_call | solution.py:64
  20.9 3.4 %collective-permute-done.1.refs_1_ = bf16[1024,128]{1,0:T(8,128)(2,1)S(1)} collective-permute-done((bf16[1024,128]{1,0:T(8,128)(2,1)}, bf16[1024,128]{1,0:T(8,128)(2,1)S(1)}, u32[]{:S(2)}, u32[]{:S(2)}) %collective-permute-start.1) | collective-permute-done | bytes 262176 | tf_op jit(solution)/shard_map/ppermute | solution.py:272
  24.3 1.9 %collective-permute-start.2 = (bf16[1024,128]{1,0:T(8,128)(2,1)S(1)}, bf16[1024,128]{1,0:T(8,128)(2,1)S(1)}, u32[]{:S(2)}, u32[]{:S(2)}) collective-permute-start(bf16[1024,128]{1,0:T(8,128)(2,1)S(1)} %collective-permute-done.1.refs_1_), channel_id=1, source_target_pairs={{0,16},{1,17},{2,18},{3,19},{4,20},{5,21},{6,22},{7,23},{8,24},{9,... | collective-permute-start | bytes 786440 | tf_op jit(solution)/shard_map/ppermute | solution.py:272
  26.3 13.1 %collective-permute-done.refs_3_ = bf16[1024,128]{1,0:T(8,128)(2,1)S(1)} collective-permute-done((bf16[1024,128]{1,0:T(8,128)(2,1)}, bf16[1024,128]{1,0:T(8,128)(2,1)S(1)}, u32[]{:S(2)}, u32[]{:S(2)}) %collective-permute-start) | collective-permute-done | bytes 262176 | tf_op jit(solution)/shard_map/ppermute | solution.py:272
  39.4 1.9 %collective-permute-start.3 = (bf16[1024,128]{1,0:T(8,128)(2,1)S(1)}, bf16[1024,128]{1,0:T(8,128)(2,1)S(1)}, u32[]{:S(2)}, u32[]{:S(2)}) collective-permute-start(bf16[1024,128]{1,0:T(8,128)(2,1)S(1)} %collective-permute-done.refs_3_), channel_id=1, source_target_pairs={{0,16},{1,17},{2,18},{3,19},{4,20},{5,21},{6,22},{7,23},{8,24},{9,... | collective-permute-start | bytes 786440 | tf_op jit(solution)/shard_map/ppermute | solution.py:272
  41.3 4.7 %count_tiles.3.far_ref = bf16[2048,1024]{1,0:T(8,128)(2,1)S(1)} custom-call(s32[10,1024]{1,0:T(8,128)S(1)} %bitcast.5), custom_call_target="tpu_custom_call" | custom-call | flops 62914560 | bytes 4194304 | tf_op jit(solution)/shard_map/count_tiles/pallas_call | solution.py:64
  46.0 0.0 copy-start.3
  46.0 0.0 copy-start.6
  46.0 1.3 %gather_sum.1.part_ref = f32[128,1024]{1,0:T(8,128)S(1)} custom-call(bf16[3072,1024]{1,0:T(8,128)(2,1)S(1)} %count_tiles.2.close_ref, bf16[2048,1024]{1,0:T(8,128)(2,1)S(1)} %count_tiles.3.far_ref, bf16[1024,128]{1,0:T(8,128)(2,1)S(1)} %copy-done.2, bf16[1024,128]{1,0:T(8,128)(2,1)S(1)} %collective-permute-done.1.refs_1_, ...), custom_call_target="tpu_custom_call" | custom-call | flops 1073741824 | bytes 1048576 | tf_op jit(solution)/shard_map/gather_sum/pallas_call | solution.py:99
  47.4 2.4 %collective-permute-done.3.block_ref = bf16[1024,128]{1,0:T(8,128)(2,1)S(1)} collective-permute-done((bf16[1024,128]{1,0:T(8,128)(2,1)S(1)}, bf16[1024,128]{1,0:T(8,128)(2,1)S(1)}, u32[]{:S(2)}, u32[]{:S(2)}) %collective-permute-start.3) | collective-permute-done | bytes 262176 | tf_op jit(solution)/shard_map/ppermute | solution.py:272
  49.8 4.6 %layer.1 = (bf16[1024,512]{1,0:T(8,128)(2,1)}, bf16[64,24,128]{2,1,0:T(8,128)(2,1)}, f32[1024,128]{1,0:T(8,128)S(1)}, bf16[1024,128]{1,0:T(8,128)(2,1)S(1)}, bf16[2048,128]{1,0:T(8,128)(2,1)S(1)}) custom-call(bf16[3072,1024]{1,0:T(8,128)(2,1)S(1)} %count_tiles.2.close_ref, bf16[2048,1024]{1,0:T(8,128)(2,1)S(1)} %count_tiles.3.far_ref, ...), custom_call_target="tpu_custom_call" | custom-call | flops 1610612736 | bytes 2097152 | tf_op jit(solution)/shard_map/layer/pallas_call | solution.py:194
  54.4 7.9 %all-to-all-start = ((bf16[64,24,128]{2,1,0:T(8,128)(2,1)}), bf16[64,24,128]{2,1,0:T(8,128)(2,1)S(1)}, u32[]{:S(2)}, u32[]{:S(2)}) async-start(bf16[64,24,128]{2,1,0:T(8,128)(2,1)} %get-tuple-element.31), calls=%async_computation | async-start | bytes 786432 | tf_op jit(solution)/shard_map/all_to_all | solution.py:276
  62.4 5.2 %collective-permute-start.4 = (bf16[2048,128]{1,0:T(8,128)(2,1)S(1)}, bf16[2048,128]{1,0:T(8,128)(2,1)S(1)}, u32[]{:S(2)}, u32[]{:S(2)}) collective-permute-start(bf16[2048,128]{1,0:T(8,128)(2,1)S(1)} %get-tuple-element.30), channel_id=1, source_target_pairs={{0,752},{1,753},{2,754},{3,755},{4,756},{5,757},{6,758},{7,759},{8... | collective-permute-start | bytes 1572872 | tf_op jit(solution)/shard_map/ppermute | solution.py:272
  67.6 2.8 %copy-done.1 = bf16[3072,1024]{1,0:T(8,128)(2,1)S(1)} copy-done((bf16[3072,1024]{1,0:T(8,128)(2,1)S(1)}, bf16[3072,1024]{1,0:T(8,128)(2,1)}, u32[]{:S(2)}) %copy-start.1) | copy-done | bytes 6291480
  70.3 1.8 %spread.1 = (f32[1024,128]{1,0:T(8,128)S(1)}, bf16[2048,128]{1,0:T(8,128)(2,1)S(1)}) custom-call(bf16[3072,1024]{1,0:T(8,128)(2,1)S(1)} %copy-done.1, bf16[1024,128]{1,0:T(8,128)(2,1)S(1)} %get-tuple-element.26.dmean_ref, f32[1024,128]{1,0:T(8,128)S(1)} %get-tuple-element.27.dself_ref), custom_call_target="tpu_custom_call" | custom-call | flops 805306368 | bytes 786432 | tf_op jit(solution)/shard_map/spread/pallas_call | solution.py:225
  72.1 5.0 %all-to-all-done = bf16[64,24,128]{2,1,0:T(8,128)(2,1)S(1)} async-done(((bf16[64,24,128]{2,1,0:T(8,128)(2,1)}), bf16[64,24,128]{2,1,0:T(8,128)(2,1)S(1)}, u32[]{:S(2)}, u32[]{:S(2)}) %all-to-all-start) | async-done | bytes 393248 | tf_op jit(solution)/shard_map/all_to_all | solution.py:276
  77.1 0.1 reduce_sum.21
  77.2 0.6 broadcast_in_dim.7
  77.8 3.8 %all-to-all-start.1 = ((bf16[12,24,128]{2,1,0:T(8,128)(2,1)}), bf16[12,24,128]{2,1,0:T(8,128)(2,1)S(1)}, u32[]{:S(2)}, u32[]{:S(2)}) async-start(bf16[12,24,128]{2,1,0:T(8,128)(2,1)} %broadcast_in_dim.7), calls=%async_computation.1 | async-start | bytes 147456 | tf_op jit(solution)/shard_map/all_to_all | solution.py:276
  81.6 0.1 add_convert_fusion
  81.8 9.9 %collective-permute-start.5 = (bf16[1024,128]{1,0:T(8,128)(2,1)S(1)}, bf16[1024,128]{1,0:T(8,128)(2,1)S(1)}, u32[]{:S(2)}, u32[]{:S(2)}) collective-permute-start(bf16[1024,128]{1,0:T(8,128)(2,1)S(1)} %get-tuple-element.35), channel_id=1, source_target_pairs={{0,760},{1,761},{2,762},{3,763},{4,764},{5,765},{6,766},{7,767},{8... | collective-permute-start | bytes 786440 | tf_op jit(solution)/shard_map/ppermute | solution.py:272
  91.8 1.9 %collective-permute-start.6 = (bf16[1024,128]{1,0:T(8,128)(2,1)S(1)}, bf16[1024,128]{1,0:T(8,128)(2,1)S(1)}, u32[]{:S(2)}, u32[]{:S(2)}) collective-permute-start(bf16[1024,128]{1,0:T(8,128)(2,1)S(1)} %get-tuple-element.36), channel_id=1, source_target_pairs={{0,752},{1,753},{2,754},{3,755},{4,756},{5,757},{6,758},{7,759},{8... | collective-permute-start | bytes 786440 | tf_op jit(solution)/shard_map/ppermute | solution.py:272
  93.7 0.7 broadcast_in_dim.8
  94.5 5.8 %all-to-all-start.2 = ((bf16[64,16,128]{2,1,0:T(8,128)(2,1)}), bf16[64,16,128]{2,1,0:T(8,128)(2,1)S(1)}, u32[]{:S(2)}, u32[]{:S(2)}) async-start(bf16[64,16,128]{2,1,0:T(8,128)(2,1)} %broadcast_in_dim.8), calls=%async_computation.2 | async-start | bytes 524288 | tf_op jit(solution)/shard_map/all_to_all | solution.py:276
  100.3 0.6 slice_bitcast_fusion
  100.9 1.7 %collective-permute-done.6 = bf16[1024,128]{1,0:T(8,128)(2,1)S(1)} collective-permute-done((bf16[1024,128]{1,0:T(8,128)(2,1)S(1)}, bf16[1024,128]{1,0:T(8,128)(2,1)S(1)}, u32[]{:S(2)}, u32[]{:S(2)}) %collective-permute-start.6) | collective-permute-done | bytes 262176 | tf_op jit(solution)/shard_map/ppermute | solution.py:272
  102.6 0.8 add_convert_fusion.1
  103.4 8.9 %all-to-all-done.2.chunks_ref = bf16[64,16,128]{2,1,0:T(8,128)(2,1)S(1)} async-done(((bf16[64,16,128]{2,1,0:T(8,128)(2,1)}), bf16[64,16,128]{2,1,0:T(8,128)(2,1)S(1)}, u32[]{:S(2)}, u32[]{:S(2)}) %all-to-all-start.2) | async-done | bytes 262176 | tf_op jit(solution)/shard_map/all_to_all | solution.py:276
  112.3 0.8 unfold.1
  (20 shorter events, 0.1 us)
Async XLA Ops:
  0.6 45.4 %copy-start.2 = (bf16[1024,128]{1,0:T(8,128)(2,1)S(1)}, bf16[1024,128]{1,0:T(8,128)(2,1)}, u32[]{:S(2)}) copy-start(bf16[1024,128]{1,0:T(8,128)(2,1)} %own_ref.1) | copy-start | bytes 786436
  0.6 23.7 %collective-permute-start.1 = (bf16[1024,128]{1,0:T(8,128)(2,1)}, bf16[1024,128]{1,0:T(8,128)(2,1)S(1)}, u32[]{:S(2)}, u32[]{:S(2)}) collective-permute-start(bf16[1024,128]{1,0:T(8,128)(2,1)} %own_ref.1), channel_id=1, source_target_pairs={{0,16},{1,17},{2,18},{3,19},{4,20},{5,21},{6,22},{7,23},{8,24},{9,... | collective-permute-start | bytes 786440 | tf_op jit(solution)/shard_map/ppermute | solution.py:272
  5.6 33.8 %collective-permute-start = (bf16[1024,128]{1,0:T(8,128)(2,1)}, bf16[1024,128]{1,0:T(8,128)(2,1)S(1)}, u32[]{:S(2)}, u32[]{:S(2)}) collective-permute-start(bf16[1024,128]{1,0:T(8,128)(2,1)} %own_ref.1), channel_id=1, source_target_pairs={{0,8},{1,9},{2,10},{3,11},{4,12},{5,13},{6,14},{7,15},{8,16},{9,17... | collective-permute-start | bytes 786440 | tf_op jit(solution)/shard_map/ppermute | solution.py:272
  13.1 0.8 copy-start.4
  20.9 28.9 %copy-start = (bf16[3072,1024]{1,0:T(8,128)(2,1)}, bf16[3072,1024]{1,0:T(8,128)(2,1)S(1)}, u32[]{:S(2)}) copy-start(bf16[3072,1024]{1,0:T(8,128)(2,1)S(1)} %count_tiles.2.close_ref) | copy-start | bytes 18874372
  24.3 21.7 %collective-permute-start.2 = (bf16[1024,128]{1,0:T(8,128)(2,1)S(1)}, bf16[1024,128]{1,0:T(8,128)(2,1)S(1)}, u32[]{:S(2)}, u32[]{:S(2)}) collective-permute-start(bf16[1024,128]{1,0:T(8,128)(2,1)S(1)} %collective-permute-done.1.refs_1_), channel_id=1, source_target_pairs={{0,16},{1,17},{2,18},{3,19},{4,20},{5,21},{6,22},{7,23},{8,24},{9,... | collective-permute-start | bytes 786440 | tf_op jit(solution)/shard_map/ppermute | solution.py:272
  39.4 10.4 %collective-permute-start.3 = (bf16[1024,128]{1,0:T(8,128)(2,1)S(1)}, bf16[1024,128]{1,0:T(8,128)(2,1)S(1)}, u32[]{:S(2)}, u32[]{:S(2)}) collective-permute-start(bf16[1024,128]{1,0:T(8,128)(2,1)S(1)} %collective-permute-done.refs_3_), channel_id=1, source_target_pairs={{0,16},{1,17},{2,18},{3,19},{4,20},{5,21},{6,22},{7,23},{8,24},{9,... | collective-permute-start | bytes 786440 | tf_op jit(solution)/shard_map/ppermute | solution.py:272
  46.0 3.8 %copy-start.3 = (bf16[1024,512]{1,0:T(8,128)(2,1)S(1)}, bf16[1024,512]{1,0:T(8,128)(2,1)}, u32[]{:S(2)}) copy-start(bf16[1024,512]{1,0:T(8,128)(2,1)} %cot_ref.1) | copy-start | bytes 3145732
  46.0 3.8 %copy-start.5 = (bf16[128,512]{1,0:T(8,128)(2,1)S(1)}, bf16[128,512]{1,0:T(8,128)(2,1)}, u32[]{:S(2)}) copy-start(bf16[128,512]{1,0:T(8,128)(2,1)} %w_self_ref.1) | copy-start | bytes 393220
  46.0 3.8 %copy-start.6 = (bf16[128,512]{1,0:T(8,128)(2,1)S(1)}, bf16[128,512]{1,0:T(8,128)(2,1)}, u32[]{:S(2)}) copy-start(bf16[128,512]{1,0:T(8,128)(2,1)} %w_neigh_ref.1) | copy-start | bytes 393220
  46.0 3.8 %copy-start.7 = (f32[512]{0:T(512)S(1)}, f32[512]{0:T(512)}, u32[]{:S(2)}) copy-start(f32[512]{0:T(512)} %param.10) | copy-start | bytes 6148
  54.4 22.7 %all-to-all-start = ((bf16[64,24,128]{2,1,0:T(8,128)(2,1)}), bf16[64,24,128]{2,1,0:T(8,128)(2,1)S(1)}, u32[]{:S(2)}, u32[]{:S(2)}) async-start(bf16[64,24,128]{2,1,0:T(8,128)(2,1)} %get-tuple-element.31), calls=%async_computation | async-start | bytes 786432 | tf_op jit(solution)/shard_map/all_to_all | solution.py:276
  62.4 19.2 %collective-permute-start.4 = (bf16[2048,128]{1,0:T(8,128)(2,1)S(1)}, bf16[2048,128]{1,0:T(8,128)(2,1)S(1)}, u32[]{:S(2)}, u32[]{:S(2)}) collective-permute-start(bf16[2048,128]{1,0:T(8,128)(2,1)S(1)} %get-tuple-element.30), channel_id=1, source_target_pairs={{0,752},{1,753},{2,754},{3,755},{4,756},{5,757},{6,758},{7,759},{8... | collective-permute-start | bytes 1572872 | tf_op jit(solution)/shard_map/ppermute | solution.py:272
  67.6 2.8 %copy-start.1 = (bf16[3072,1024]{1,0:T(8,128)(2,1)S(1)}, bf16[3072,1024]{1,0:T(8,128)(2,1)}, u32[]{:S(2)}) copy-start(bf16[3072,1024]{1,0:T(8,128)(2,1)} %copy-done) | copy-start | bytes 18874372
  77.8 15.9 %all-to-all-start.1 = ((bf16[12,24,128]{2,1,0:T(8,128)(2,1)}), bf16[12,24,128]{2,1,0:T(8,128)(2,1)S(1)}, u32[]{:S(2)}, u32[]{:S(2)}) async-start(bf16[12,24,128]{2,1,0:T(8,128)(2,1)} %broadcast_in_dim.7), calls=%async_computation.1 | async-start | bytes 147456 | tf_op jit(solution)/shard_map/all_to_all | solution.py:276
  81.8 19.1 %collective-permute-start.5 = (bf16[1024,128]{1,0:T(8,128)(2,1)S(1)}, bf16[1024,128]{1,0:T(8,128)(2,1)S(1)}, u32[]{:S(2)}, u32[]{:S(2)}) collective-permute-start(bf16[1024,128]{1,0:T(8,128)(2,1)S(1)} %get-tuple-element.35), channel_id=1, source_target_pairs={{0,760},{1,761},{2,762},{3,763},{4,764},{5,765},{6,766},{7,767},{8... | collective-permute-start | bytes 786440 | tf_op jit(solution)/shard_map/ppermute | solution.py:272
  91.8 10.8 %collective-permute-start.6 = (bf16[1024,128]{1,0:T(8,128)(2,1)S(1)}, bf16[1024,128]{1,0:T(8,128)(2,1)S(1)}, u32[]{:S(2)}, u32[]{:S(2)}) collective-permute-start(bf16[1024,128]{1,0:T(8,128)(2,1)S(1)} %get-tuple-element.36), channel_id=1, source_target_pairs={{0,752},{1,753},{2,754},{3,755},{4,756},{5,757},{6,758},{7,759},{8... | collective-permute-start | bytes 786440 | tf_op jit(solution)/shard_map/ppermute | solution.py:272
  94.5 17.8 %all-to-all-start.2 = ((bf16[64,16,128]{2,1,0:T(8,128)(2,1)}), bf16[64,16,128]{2,1,0:T(8,128)(2,1)S(1)}, u32[]{:S(2)}, u32[]{:S(2)}) async-start(bf16[64,16,128]{2,1,0:T(8,128)(2,1)} %broadcast_in_dim.8), calls=%async_computation.2 | async-start | bytes 524288 | tf_op jit(solution)/shard_map/all_to_all | solution.py:276
